TPU v7x, 32 devices: a whole 2x2x4 slice. The times are simulated.
32 devices in a mesh: shard: 2 (over x), tm: 16 (over z, y, core).
Axes of the slice: x: 2, y: 2, z: 4, core: 2. Of those that a mesh axis runs over, the one named last changes fastest.
Arguments:
- latents: bfloat16 [128, 32, 1536], P(('shard', 'tm')), parts along dimension 0, as said below
- w_query: bfloat16 [1536, 1536], replicated, may hold values from -0.15625 to 0.15625
- w_key: bfloat16 [1536, 1536], replicated, may hold values from -0.15625 to 0.15625
- w_value: bfloat16 [1536, 1536], replicated, may hold values from -0.15625 to 0.15625
- w_out: bfloat16 [1536, 1536], replicated, may hold values from -0.15625 to 0.15625
- cotangent: bfloat16 [128, 32, 1536], P(('shard', 'tm')), parts along dimension 0, may hold values from -6 to 6
- memory_ids: int32 [128, 4], P(('shard', 'tm')), parts along dimension 0, may hold values from 0 to 63, as said below
- memory_count: int32 [128], P(('shard', 'tm')), parts along dimension 0, may hold values from 1 to 4
- tile_mask: int32 [128, 2], P(('shard', 'tm')), parts along dimension 0, may hold values 0 or 1
Outputs:
- layer_out: bfloat16 [128, 32, 1536], P(('shard', 'tm')), parts along dimension 0
- latent_grad: bfloat16 [128, 32, 1536], P(('shard', 'tm')), parts along dimension 0
There are 2 independent parts, one for each index of `shard`. A program takes and returns all parts, laid end to end along the dimension named above; an argument that names none is the same for every part. Nothing has to cross between parts.
Inputs may be any that keep to these rules, and one draw needn't show every extreme that they name: `memory_ids`: the 16 entries of the frames of one aligned block of 4 frames (frames b * 4 to b * 4 + 3) lie in 16 different such blocks. `latents`: entries lie between -40 and 40.
All inputs are finite; a program needn't handle non-finite values. No bound on the sum of `tile_mask` on one device may be relied on, other than what follows from the above.
Results may differ from a plain program's by a relative error of at most 0.014.
The roundings to bfloat16 on the way count: a program that leaves them out, or rounds other values in their place, can miss the bound.
Values may be sent and summed in bfloat16 or wider, within the bound.
A program may use at most 192 MiB of HBM per device.

v0:
```python
import functools
import math

import jax
import jax.numpy as jnp
from jax import lax
from jax.experimental import pallas as pl
from jax.experimental.pallas import tpu as pltpu
from jax.sharding import PartitionSpec as P

HEADS = 24
GROUP = 4
NT = (((1,), (1,)), ((), ()))
NN = (((1,), (0,)), ((), ()))
TN = (((0,), (0,)), ((), ()))
MESH = pl.DeviceIdType.MESH


def dot(a, b, dims):
    return lax.dot_general(a, b, dims, preferred_element_type=jnp.float32)


CHUNK = 8


def layer_kernel(
    count, frames, mem, tile, head_dim, steps,
    spots, place, wanted, recalled, tiles, x_ref, cot_ref,
    wq_hbm, wo_hbm, wk_hbm, wv_hbm,
    layer_ref, grad_ref,
    weights, q_ref, g_ref, k_ext, v_ext, k_mem, v_mem, want_out, want_in, choose, rows_out, rows_in,
    mixed, query_grad, sums, blocks, outgoing, incoming, total,
    weight_sem, want_send, want_recv, row_send, row_recv, halo_send, halo_recv,
    send_sem, recv_sem, edge_send, edge_recv,
):
    me = lax.axis_index("tm")
    width = q_ref.shape[1]
    own = q_ref.shape[0]
    cols = width // steps
    wide = 2 * cols
    rows = GROUP * tile
    inv_root = 1.0 / math.sqrt(head_dim)
    loads = [
        pltpu.make_async_copy(source, weights.at[i], weight_sem.at[i])
        for i, source in enumerate((wq_hbm, wo_hbm, wk_hbm, wv_hbm))
    ]
    for load in loads:
        load.start()

    def shift(i):
        half = i // 2
        return count // 2 + (i % 2) * 2 * half - half

    def peer(i):
        return {"tm": lax.rem(me + shift(i), count)}

    def asker(i):
        return {"tm": lax.rem(me + count - shift(i), count)}

    def beside(side):
        return {"tm": lax.rem(me + (1 if side == 0 else count - 1), count)}

    barrier = pltpu.get_barrier_semaphore()

    @pl.loop(1, count)
    def _(i):
        pl.semaphore_signal(barrier, inc=1, device_id=peer(i), device_id_type=MESH)

    @pl.loop(0, count)
    def _(i):
        want_out[i] = jnp.full((8, own), wanted[i], jnp.int32)

    pl.semaphore_wait(barrier, count - 1)

    def ask(i):
        return pltpu.make_async_remote_copy(
            src_ref=want_out.at[i], dst_ref=want_in.at[i], send_sem=want_send,
            recv_sem=want_recv, device_id=peer(i), device_id_type=MESH,
        )

    def push_halo(side):
        return pltpu.make_async_remote_copy(
            src_ref=x_ref.at[pl.ds((frames - 1) * tile if side == 0 else 0, tile)],
            dst_ref=rows_in.at[count + side],
            send_sem=halo_send.at[side], recv_sem=halo_recv.at[side],
            device_id=beside(side), device_id_type=MESH,
        )

    def push_row(i, c):
        return pltpu.make_async_remote_copy(
            src_ref=rows_out.at[i], dst_ref=rows_in.at[i], send_sem=row_send,
            recv_sem=row_recv.at[c], device_id=asker(i), device_id_type=MESH,
        )

    @pl.loop(1, count)
    def _(i):
        ask(i).start()

    push_halo(0).start()
    push_halo(1).start()
    want_in[0] = want_out[0]
    others = pl.ds(1, count - 1)
    pltpu.make_async_copy(want_in.at[others], want_in.at[others], want_recv).wait()

    chunks = count // CHUNK
    shape = (CHUNK, tile, own)
    token = lax.broadcasted_iota(jnp.int32, shape, 1)
    lane = lax.broadcasted_iota(jnp.int32, shape, 2)

    def pick_rows(c):
        asked = want_in[pl.ds(c * CHUNK, CHUNK)][:, 0:1, :]
        hot = jnp.where(lane == asked * tile + token, 1.0, 0.0).astype(jnp.bfloat16)
        hot = hot.reshape(CHUNK * tile, own)
        choose[pl.ds(pl.multiple_of(c * (CHUNK * tile), CHUNK * tile), CHUNK * tile), :] = hot
        for part in range(width // wide):
            lanes = slice(part * wide, (part + 1) * wide)
            rows_out[pl.ds(c * CHUNK, CHUNK), :, lanes] = (
                dot(hot, x_ref[:, lanes], NN).astype(jnp.bfloat16).reshape(CHUNK, tile, wide)
            )

    pick_rows(0)

    @pl.loop(1, CHUNK)
    def _(i):
        push_row(i, 0).start()

    rows_in[0] = rows_out[0]

    @pl.loop(1, chunks)
    def _(c):
        pick_rows(c)

        @pl.loop(0, CHUNK)
        def _(i):
            push_row(c * CHUNK + i, c).start()

    edge_row = lax.broadcasted_iota(jnp.int32, (2 * tile, own), 0)
    edge_lane = lax.broadcasted_iota(jnp.int32, (2 * tile, own), 1)
    edge_spot = jnp.where(edge_row < tile, edge_row, edge_row + (frames - 2) * tile)
    choose[count * tile : (count + 2) * tile, :] = jnp.where(
        edge_lane == edge_spot, 1.0, 0.0
    ).astype(jnp.bfloat16)

    loads[0].wait()

    @pl.loop(0, width // wide)
    def _(p):
        lanes = pl.ds(pl.multiple_of(p * wide, wide), wide)
        q_ref[:, lanes] = dot(x_ref[...], weights[0, :, lanes], NN).astype(jnp.bfloat16)

    loads[1].wait()

    @pl.loop(0, width // wide)
    def _(p):
        lanes = pl.ds(pl.multiple_of(p * wide, wide), wide)
        g_ref[:, lanes] = dot(cot_ref[...], weights[1, lanes, :], NT).astype(jnp.bfloat16)

    push_halo(0).wait_recv()
    push_halo(1).wait_recv()
    loads[2].wait()
    loads[3].wait()

    @pl.loop(0, width // wide)
    def _(p):
        lanes = pl.ds(pl.multiple_of(p * wide, wide), wide)
        ext = jnp.concatenate([rows_in[count], x_ref[...], rows_in[count + 1]], axis=0)
        k_ext[:, lanes] = dot(ext, weights[2, :, lanes], NN).astype(jnp.bfloat16)
        v_ext[:, lanes] = dot(ext, weights[3, :, lanes], NN).astype(jnp.bfloat16)

    def project(c):
        some = pl.ds(c * CHUNK, CHUNK)

        @pl.loop(0, width // wide)
        def _(p):
            lanes = pl.ds(pl.multiple_of(p * wide, wide), wide)
            flat = rows_in[some].reshape(CHUNK * tile, width)
            for weight, far in ((2, k_mem), (3, v_mem)):
                far[some, :, lanes] = (
                    dot(flat, weights[weight, :, lanes], NN)
                    .astype(jnp.bfloat16)
                    .reshape(CHUNK, tile, wide)
                )

    first = pl.ds(1, CHUNK - 1)
    pltpu.make_async_copy(rows_in.at[first], rows_in.at[first], row_recv.at[0]).wait()
    project(0)

    @pl.loop(1, chunks)
    def _(c):
        some = pl.ds(c * CHUNK, CHUNK)
        pltpu.make_async_copy(rows_in.at[some], rows_in.at[some], row_recv.at[c]).wait()
        project(c)

    own_head = (
        lax.broadcasted_iota(jnp.int32, (rows, cols), 0) // tile
        == lax.broadcasted_iota(jnp.int32, (rows, cols), 1) // head_dim
    )

    def spread(block):
        tall = jnp.concatenate([block] * GROUP, axis=0)
        return jnp.where(own_head, tall, jnp.zeros_like(tall))

    def fold(tall):
        tall = jnp.where(own_head, tall, 0.0)
        flat = tall[0:tile]
        for part in range(1, GROUP):
            flat = flat + tall[part * tile : (part + 1) * tile]
        return flat

    def push(g, d):
        return pltpu.make_async_remote_copy(
            src_ref=outgoing.at[g, d],
            dst_ref=incoming.at[g, d],
            send_sem=send_sem.at[g],
            recv_sem=recv_sem.at[g],
            device_id=peer(d),
            device_id_type=MESH,
        )

    def push_edge(g, side):
        return pltpu.make_async_remote_copy(
            src_ref=outgoing.at[g, count + side],
            dst_ref=incoming.at[g, count + side],
            send_sem=edge_send.at[g, side],
            recv_sem=edge_recv.at[g, side],
            device_id=beside(side),
            device_id_type=MESH,
        )

    block_of = lax.broadcasted_iota(jnp.int32, (1, (3 + mem) * tile), 1) // tile

    def valid(f):
        frame = me * frames + f
        lower = jnp.where(frame >= 1, tiles[f, 0], 0)
        upper = jnp.where(frame < frames * count - 1, tiles[f, 1], 0)
        near = jnp.where(block_of == 0, lower, jnp.where(block_of == 1, 1, upper))
        kept = jnp.where(block_of - 3 < recalled[f], 1, 0)
        return jnp.where(block_of < 3, near, kept) > 0

    def attend(g):
        lanes = pl.ds(pl.multiple_of(g * cols, cols), cols)
        for f in range(frames):
            here = slice(f * tile, (f + 1) * tile)
            near = slice(f * tile, (f + 3) * tile)

            def gather(ext, far):
                return jnp.concatenate(
                    [ext[near, lanes]] + [far[spots[f * mem + j], :, lanes] for j in range(mem)],
                    axis=0,
                )

            keys = gather(k_ext, k_mem)
            values = gather(v_ext, v_mem)
            queries = spread(q_ref[here, lanes])
            grads = spread(g_ref[here, lanes])
            scores = dot(queries, keys, NT) * inv_root
            scores = jnp.where(valid(f), scores, -1e30)
            expo = jnp.exp(scores - jnp.max(scores, axis=-1, keepdims=True))
            prob = expo / jnp.sum(expo, axis=-1, keepdims=True)
            low = prob.astype(jnp.bfloat16)
            mixed[here, lanes] = fold(dot(low, values, NN)).astype(jnp.bfloat16)
            prob_grad = dot(grads, values, NT)
            delta = jnp.sum(prob * prob_grad, axis=-1, keepdims=True)
            score_grad = (prob * (prob_grad - delta) * inv_root).astype(jnp.bfloat16)
            query_grad[here, lanes] = fold(dot(score_grad, keys, NN)).astype(jnp.bfloat16)
            parts = (
                dot(score_grad, queries, TN).astype(jnp.bfloat16),
                dot(low, grads, TN).astype(jnp.bfloat16),
            )
            for kv, part in enumerate(parts):
                before = part[0:tile]
                own = part[tile : 2 * tile].astype(jnp.float32)
                after = part[2 * tile : 3 * tile]
                if f == 0:
                    outgoing[g, count + 1, kv] = before
                    sums[kv, here, lanes] = own
                else:
                    back = slice((f - 1) * tile, f * tile)
                    sums[kv, back, lanes] += before.astype(jnp.float32)
                    sums[kv, here, lanes] += own
                if f == frames - 1:
                    outgoing[g, count, kv] = after
                else:
                    ahead = slice((f + 1) * tile, (f + 2) * tile)
                    sums[kv, ahead, lanes] = after.astype(jnp.float32)
                for j in range(mem):
                    blocks[f * mem + j, kv] = part[(3 + j) * tile : (4 + j) * tile]

    def send(g):
        @pl.loop(1, count)
        def _(d):
            outgoing[g, d] = blocks[place[d]]
            push(g, d).start()

        push_edge(g, 0).start()
        push_edge(g, 1).start()
        incoming[g, 0] = blocks[place[0]]

    @pl.loop(0, steps)
    def _(g):
        attend(g)
        send(g)

    for part in range(width // wide):
        lanes = slice(part * wide, (part + 1) * wide)
        layer_ref[:, lanes] = dot(mixed[...], weights[1, :, lanes], NN).astype(jnp.bfloat16)
        total[:, lanes] = dot(query_grad[...], weights[0, lanes, :], NT)

    @pl.loop(0, steps)
    def _(g):
        lanes = pl.ds(pl.multiple_of(g * cols, cols), cols)
        pltpu.make_async_copy(incoming.at[g, others], incoming.at[g, others], recv_sem.at[g]).wait()
        push_edge(g, 0).wait_recv()
        push_edge(g, 1).wait_recv()
        for kv in range(2):
            came = incoming[g, :, kv].reshape((count + 2) * tile, cols)
            whole = sums[kv, :, lanes] + dot(choose[...], came, TN)
            total[...] += dot(whole.astype(jnp.bfloat16), weights[2 + kv, :, lanes], NT)

    grad_ref[...] = total[...].astype(jnp.bfloat16)
    pltpu.make_async_copy(want_out.at[others], want_out.at[others], want_send).wait()
    pltpu.make_async_copy(rows_out.at[others], rows_out.at[others], row_send).wait()
    push_halo(0).wait_send()
    push_halo(1).wait_send()

    @pl.loop(0, steps)
    def _(g):
        pltpu.make_async_copy(outgoing.at[g, others], outgoing.at[g, others], send_sem.at[g]).wait()
        push_edge(g, 0).wait_send()
        push_edge(g, 1).wait_send()


def on_device(
    latents, w_query, w_key, w_value, w_out, cotangent, memory_ids, memory_count, tile_mask
):
    frames, tile, width = latents.shape
    count = lax.axis_size("tm")
    me = lax.axis_index("tm")
    rows = latents.reshape(-1, width)
    mem = memory_ids.shape[1]
    inner = w_query.shape[1]
    head_dim = inner // HEADS
    cols = GROUP * head_dim
    steps = inner // cols
    order = jnp.arange(count, dtype=jnp.int32)
    half = order // 2
    shift = jnp.where(order == 0, 0, count // 2 + jnp.where(order % 2 == 1, half, -half))
    targets = (me + shift) % count

    owners = (memory_ids // frames).reshape(1, -1).astype(jnp.int32)
    local = (memory_ids % frames).reshape(1, -1).astype(jnp.int32)
    entry = jnp.arange(frames * mem, dtype=jnp.int32)
    spots = jnp.sum(jnp.where(targets[:, None] == owners, order[:, None], 0), axis=0)
    spots = spots.astype(jnp.int32)
    matched = targets[:, None] == owners
    place = jnp.sum(jnp.where(matched, entry[None, :], 0), axis=1).astype(jnp.int32)
    wanted = jnp.sum(jnp.where(matched, local + 1, 0), axis=1).astype(jnp.int32) - 1
    own = frames * tile
    wanted = jnp.where(wanted < 0, -frames, wanted)

    vmem = pl.BlockSpec(memory_space=pltpu.VMEM)
    smem = pl.BlockSpec(memory_space=pltpu.SMEM)
    hbm = pl.BlockSpec(memory_space=pl.ANY)
    block = (2, tile, cols)
    layer_out, latent_grad = pl.pallas_call(
        functools.partial(layer_kernel, count, frames, mem, tile, head_dim, steps),
        in_specs=[smem] * 5 + [vmem] * 2 + [hbm] * 4,
        out_specs=[vmem, vmem],
        out_shape=[
            jax.ShapeDtypeStruct((own, width), jnp.bfloat16),
            jax.ShapeDtypeStruct((own, width), jnp.bfloat16),
        ],
        scratch_shapes=[
            pltpu.VMEM((4, width, inner), jnp.bfloat16),
            pltpu.VMEM((own, inner), jnp.bfloat16),
            pltpu.VMEM((own, inner), jnp.bfloat16),
            pltpu.VMEM((own + 2 * tile, inner), jnp.bfloat16),
            pltpu.VMEM((own + 2 * tile, inner), jnp.bfloat16),
            pltpu.VMEM((count, tile, inner), jnp.bfloat16),
            pltpu.VMEM((count, tile, inner), jnp.bfloat16),
            pltpu.VMEM((count, 8, own), jnp.int32),
            pltpu.VMEM((count, 8, own), jnp.int32),
            pltpu.VMEM(((count + 2) * tile, own), jnp.bfloat16),
            pltpu.VMEM((count, tile, width), jnp.bfloat16),
            pltpu.VMEM((count + 2, tile, width), jnp.bfloat16),
            pltpu.VMEM((own, inner), jnp.bfloat16),
            pltpu.VMEM((own, inner), jnp.bfloat16),
            pltpu.VMEM((2, own, inner), jnp.float32),
            pltpu.VMEM((frames * mem,) + block, jnp.bfloat16),
            pltpu.VMEM((steps, count + 2) + block, jnp.bfloat16),
            pltpu.VMEM((steps, count + 2) + block, jnp.bfloat16),
            pltpu.VMEM((own, width), jnp.float32),
            pltpu.SemaphoreType.DMA((4,)),
            pltpu.SemaphoreType.DMA,
            pltpu.SemaphoreType.DMA,
            pltpu.SemaphoreType.DMA,
            pltpu.SemaphoreType.DMA((count // CHUNK,)),
            pltpu.SemaphoreType.DMA((2,)),
            pltpu.SemaphoreType.DMA((2,)),
            pltpu.SemaphoreType.DMA((steps,)),
            pltpu.SemaphoreType.DMA((steps,)),
            pltpu.SemaphoreType.DMA((steps, 2)),
            pltpu.SemaphoreType.DMA((steps, 2)),
        ],
        compiler_params=pltpu.CompilerParams(
            collective_id=0, has_side_effects=True, vmem_limit_bytes=58 * 2**20
        ),
    )(
        spots, place, wanted, memory_count, tile_mask, rows, cotangent.reshape(-1, width),
        w_query, w_out, w_key, w_value,
    )
    return (
        layer_out.reshape(frames, tile, width),
        latent_grad.reshape(frames, tile, width),
    )


def solution(mesh):
    placed = (
        P(("shard", "tm"), None, None),
        P(),
        P(),
        P(),
        P(),
        P(("shard", "tm"), None, None),
        P(("shard", "tm"), None),
        P(("shard", "tm")),
        P(("shard", "tm"), None),
    )
    return jax.shard_map(
        on_device,
        mesh=mesh,
        in_specs=placed,
        out_specs=(P(("shard", "tm"), None, None), P(("shard", "tm"), None, None)),
        check_vma=False,
    )
```

profile of v0, /device:TPU:16, one launch (start us, length us, event | category | flops | bytes accessed | tf_op | source)
XLA Modules:
  0.0 127.7 jit_solution(16175718389395708826)
XLA Ops:
  0.7 1.3 %copy.12.tiles = s32[4,2]{1,0:T(4,128)} copy(s32[4,2]{0,1:T(2,128)} %param.17) | data formatting | bytes 64 | tf_op args[8]
  2.0 0.7 add_select_fusion.1
  2.7 0.1 eq.44
  2.8 0.1 add.66
  2.8 0.8 fusion.2
  3.6 0.5 compare_select_fusion.3.wanted
  4.1 120.0 %shard_map.104 = (bf16[128,1536]{1,0:T(8,128)(2,1)}, bf16[128,1536]{1,0:T(8,128)(2,1)}) custom-call(s32[16]{0:T(128)} %get-tuple-element.8.spots, s32[16]{0:T(128)} %get-tuple-element.7.place, s32[16]{0:T(128)} %compare_select_fusion.3.wanted, s32[4]{0:T(128)} %recalled.1, s32[4,2]{1,0:T(4,128)} %copy.12.tiles, bf16[128,1536]{1,0:T(8,128)(2,1)} %bitcast.6, ...), custom_call_target="tpu_custom_call" | custom-call | tf_op jit(solution)/shard_map/pallas_call | solution.py:365
  124.1 1.8 %copy.15 = bf16[4,32,1536]{2,1,0:T(8,128)(2,1)} copy(bf16[4,32,1536]{2,1,0:T(8,128)(2,1)} %bitcast.5) | data formatting | bytes 786432
  125.9 1.8 %copy.16 = bf16[4,32,1536]{2,1,0:T(8,128)(2,1)} copy(bf16[4,32,1536]{2,1,0:T(8,128)(2,1)} %bitcast.4) | data formatting | bytes 786432
  (1 shorter events, 0.0 us)
where the time goes:
time: 128 us
  Pallas kernels  120 us (94%)
  local copies, waits for them, and re-layouts  5.04 us (4%)
  other arithmetic  1.95 us (2%)
    pallas_call x1, Pallas kernels, on_device(): pl.pallas_call(functools.partial(layer_kernel, count, frames, mem, tile,...  120 us
    unnamed x3, local copies, waits for them, and re-layouts  4.87 us

commit v1 on v0

v1 whole, which is shorter than its diff:
```python
import functools
import math

import jax
import jax.numpy as jnp
from jax import lax
from jax.experimental import pallas as pl
from jax.experimental.pallas import tpu as pltpu
from jax.sharding import PartitionSpec as P

HEADS = 24
GROUP = 4
CHUNK = 8
NT = (((1,), (1,)), ((), ()))
NN = (((1,), (0,)), ((), ()))
TN = (((0,), (0,)), ((), ()))
MESH = pl.DeviceIdType.MESH


def dot(a, b, dims):
    return lax.dot_general(a, b, dims, preferred_element_type=jnp.float32)


def layer_kernel(
    count, frames, mem, tile, head_dim, steps,
    ids, recalled, tiles, x_ref, cot_hbm, wq_hbm, wo_hbm, wk_hbm, wv_hbm,
    layer_ref, grad_ref,
    weights, cot_ref, q_ref, g_ref, k_ext, v_ext, k_mem, v_mem, want_out, want_in, choose,
    rows_out, rows_in, mixed, query_grad, sums, blocks, gathered, outgoing, incoming, total,
    spots, place,
    weight_sem, cot_sem, want_send, want_recv, row_send, row_recv, halo_send, halo_recv,
    send_sem, recv_sem, edge_send, edge_recv,
):
    me = lax.axis_index("tm")
    width = x_ref.shape[1]
    own = x_ref.shape[0]
    cols = q_ref.shape[1] // steps
    wide = 2 * cols
    chunks = count // CHUNK
    entries = frames * mem
    scale = 1.0 / math.sqrt(head_dim)
    loads = [
        pltpu.make_async_copy(source, weights.at[i], weight_sem.at[i])
        for i, source in enumerate((wq_hbm, wo_hbm, wk_hbm, wv_hbm))
    ]
    load_cot = pltpu.make_async_copy(cot_hbm, cot_ref, cot_sem)
    loads[0].start()
    load_cot.start()
    for load in loads[1:]:
        load.start()

    def shift(i):
        half = i // 2
        return count // 2 + (i % 2) * 2 * half - half

    def peer(i):
        return {"tm": lax.rem(me + shift(i), count)}

    def asker(i):
        return {"tm": lax.rem(me + count - shift(i), count)}

    def beside(side):
        return {"tm": lax.rem(me + (1 if side == 0 else count - 1), count)}

    barrier = pltpu.get_barrier_semaphore()

    @pl.loop(1, count)
    def _(i):
        pl.semaphore_signal(barrier, inc=1, device_id=peer(i), device_id_type=MESH)

    slots = []
    slot_at = lax.broadcasted_iota(jnp.int32, want_out.shape, 0)
    asked = jnp.full(want_out.shape, -frames, jnp.int32)
    for e in range(entries):
        frame = ids[e // mem, e % mem]
        away = lax.rem(lax.div(frame, frames) - me + count, count)
        slot = jnp.where(
            away >= count // 2, 2 * away - count + 1, lax.rem(count - 2 * away, count)
        )
        spots[e] = slot
        slots.append(slot)
        asked = jnp.where(slot_at == slot, lax.rem(frame, frames), asked)
    want_out[...] = asked

    pl.semaphore_wait(barrier, count - 1)

    def ask(i):
        return pltpu.make_async_remote_copy(
            src_ref=want_out.at[i], dst_ref=want_in.at[i], send_sem=want_send,
            recv_sem=want_recv, device_id=peer(i), device_id_type=MESH,
        )

    def push_halo(side):
        return pltpu.make_async_remote_copy(
            src_ref=x_ref.at[pl.ds((frames - 1) * tile if side == 0 else 0, tile)],
            dst_ref=rows_in.at[count + side],
            send_sem=halo_send.at[side], recv_sem=halo_recv.at[side],
            device_id=beside(side), device_id_type=MESH,
        )

    def push_row(i, c):
        return pltpu.make_async_remote_copy(
            src_ref=rows_out.at[i], dst_ref=rows_in.at[i], send_sem=row_send,
            recv_sem=row_recv.at[c], device_id=asker(i), device_id_type=MESH,
        )

    @pl.loop(1, count)
    def _(i):
        ask(i).start()

    push_halo(0).start()
    push_halo(1).start()
    want_in[0] = want_out[0]
    others = pl.ds(1, count - 1)
    pltpu.make_async_copy(want_in.at[others], want_in.at[others], want_recv).wait()

    shape = (CHUNK, tile, own)
    token = lax.broadcasted_iota(jnp.int32, shape, 1)
    lane = lax.broadcasted_iota(jnp.int32, shape, 2)

    def pick_rows(c):
        asked = want_in[pl.ds(c * CHUNK, CHUNK)][:, 0:1, :]
        hot = jnp.where(lane == asked * tile + token, 1.0, 0.0).reshape(CHUNK * tile, own)
        low = hot.astype(jnp.bfloat16)
        for part in range(width // wide):
            lanes = slice(part * wide, (part + 1) * wide)
            rows_out[pl.ds(c * CHUNK, CHUNK), :, lanes] = (
                dot(low, x_ref[:, lanes], NN).astype(jnp.bfloat16).reshape(CHUNK, tile, wide)
            )
        return hot

    hots = []
    for c in range(chunks):
        hots.append(pick_rows(c))

        @pl.loop(1 if c == 0 else 0, CHUNK)
        def _(i):
            push_row(c * CHUNK + i, c).start()

    rows_in[0] = rows_out[0]
    for c in range(chunks):
        choose[:, c * CHUNK * tile : (c + 1) * CHUNK * tile] = hots[c].T.astype(jnp.bfloat16)
    edge_row = lax.broadcasted_iota(jnp.int32, (own, 2 * tile), 0)
    edge_lane = lax.broadcasted_iota(jnp.int32, (own, 2 * tile), 1)
    edge_spot = jnp.where(edge_lane < tile, edge_lane, edge_lane + (frames - 2) * tile)
    choose[:, count * tile : (count + 2) * tile] = jnp.where(
        edge_row == edge_spot, 1.0, 0.0
    ).astype(jnp.bfloat16)

    for i in range(count):
        at = jnp.int32(0)
        for e in range(entries):
            at = jnp.where(slots[e] == i, e, at)
        place[i] = at

    loads[0].wait()

    @pl.loop(0, width // wide)
    def _(p):
        lanes = pl.ds(pl.multiple_of(p * wide, wide), wide)
        q_ref[:, lanes] = dot(x_ref[...], weights[0, :, lanes], NN).astype(jnp.bfloat16)

    load_cot.wait()
    loads[1].wait()

    @pl.loop(0, width // wide)
    def _(p):
        lanes = pl.ds(pl.multiple_of(p * wide, wide), wide)
        g_ref[:, lanes] = dot(cot_ref[...], weights[1, lanes, :], NT).astype(jnp.bfloat16)

    push_halo(0).wait_recv()
    push_halo(1).wait_recv()
    loads[2].wait()
    loads[3].wait()

    @pl.loop(0, width // wide)
    def _(p):
        lanes = pl.ds(pl.multiple_of(p * wide, wide), wide)
        ext = jnp.concatenate([rows_in[count], x_ref[...], rows_in[count + 1]], axis=0)
        k_ext[:, lanes] = dot(ext, weights[2, :, lanes], NN).astype(jnp.bfloat16)
        v_ext[:, lanes] = dot(ext, weights[3, :, lanes], NN).astype(jnp.bfloat16)

    def project(c):
        some = pl.ds(c * CHUNK, CHUNK)

        @pl.loop(0, width // wide)
        def _(p):
            lanes = pl.ds(pl.multiple_of(p * wide, wide), wide)
            flat = rows_in[some].reshape(CHUNK * tile, width)
            for weight, far in ((2, k_mem), (3, v_mem)):
                far[some, :, lanes] = (
                    dot(flat, weights[weight, :, lanes], NN)
                    .astype(jnp.bfloat16)
                    .reshape(CHUNK, tile, wide)
                )

    first = pl.ds(1, CHUNK - 1)
    pltpu.make_async_copy(rows_in.at[first], rows_in.at[first], row_recv.at[0]).wait()
    project(0)

    @pl.loop(1, chunks)
    def _(c):
        some = pl.ds(c * CHUNK, CHUNK)
        pltpu.make_async_copy(rows_in.at[some], rows_in.at[some], row_recv.at[c]).wait()
        project(c)

    rows = GROUP * tile
    own_head = (
        lax.broadcasted_iota(jnp.int32, (rows, cols), 0) // tile
        == lax.broadcasted_iota(jnp.int32, (rows, cols), 1) // head_dim
    )
    head_at = lax.broadcasted_iota(jnp.int32, (tile, cols), 1) // head_dim

    def spread(block):
        tall = jnp.concatenate([block] * GROUP, axis=0)
        return jnp.where(own_head, tall, jnp.zeros_like(tall))

    def fold(tall):
        flat = tall[0:tile]
        for part in range(1, GROUP):
            flat = jnp.where(head_at == part, tall[part * tile : (part + 1) * tile], flat)
        return flat

    def hide(f):
        frame = me * frames + f
        lower = (frame >= 1) & (tiles[0, f] == 1)
        upper = (frame < frames * count - 1) & (tiles[1, f] == 1)
        kept = [lower, None, upper] + [recalled[f] > j for j in range(mem)]
        return [None if k is None else jnp.where(k, 0.0, -1e30) for k in kept]

    def attend(g):
        lanes = pl.ds(pl.multiple_of(g * cols, cols), cols)
        held = [None, None]
        late = [None, None]
        for f in range(frames):
            here = slice(f * tile, (f + 1) * tile)
            near = slice(f * tile, (f + 3) * tile)

            def gather(ext, far):
                return jnp.concatenate(
                    [ext[near, lanes]] + [far[spots[f * mem + j], :, lanes] for j in range(mem)],
                    axis=0,
                )

            keys = gather(k_ext, k_mem)
            values = gather(v_ext, v_mem)
            queries = spread(q_ref[here, lanes] * scale)
            grads = spread(g_ref[here, lanes])
            scores = dot(keys, queries, NT)
            scores = jnp.concatenate(
                [
                    part if bias is None else part + bias
                    for bias, part in zip(hide(f), jnp.split(scores, 3 + mem, axis=0))
                ],
                axis=0,
            )
            expo = jnp.exp(scores - jnp.max(scores, axis=0, keepdims=True))
            prob = expo * (1.0 / jnp.sum(expo, axis=0, keepdims=True))
            low = prob.astype(jnp.bfloat16)
            prob_grad = dot(values, grads, NT)
            delta = jnp.sum(prob * prob_grad, axis=0, keepdims=True)
            score_grad = (prob * (prob_grad - delta)).astype(jnp.bfloat16)
            mixed[here, lanes] = fold(dot(low, values, TN)).astype(jnp.bfloat16)
            query_grad[here, lanes] = (fold(dot(score_grad, keys, TN)) * scale).astype(
                jnp.bfloat16
            )
            parts = (
                dot(score_grad, queries, NN).astype(jnp.bfloat16),
                dot(low, grads, NN).astype(jnp.bfloat16),
            )
            for kv, part in enumerate(parts):
                before = part[0:tile]
                middle = part[tile : 2 * tile].astype(jnp.float32)
                after = part[2 * tile : 3 * tile]
                if f == 0:
                    blocks[entries + 1, kv, :, lanes] = before
                else:
                    back = slice((f - 1) * tile, f * tile)
                    sums[kv, back, lanes] = (held[kv] + before.astype(jnp.float32)).astype(
                        jnp.bfloat16
                    )
                    middle = middle + late[kv]
                if f == frames - 1:
                    blocks[entries, kv, :, lanes] = after
                    sums[kv, here, lanes] = middle.astype(jnp.bfloat16)
                held[kv] = middle
                late[kv] = after.astype(jnp.float32)
                for j in range(mem):
                    blocks[f * mem + j, kv, :, lanes] = part[(3 + j) * tile : (4 + j) * tile]

    @pl.loop(0, steps)
    def _(g):
        attend(g)

    def push(i, c):
        return pltpu.make_async_remote_copy(
            src_ref=outgoing.at[i], dst_ref=incoming.at[i], send_sem=send_sem,
            recv_sem=recv_sem.at[c], device_id=peer(i), device_id_type=MESH,
        )

    def push_edge(side):
        return pltpu.make_async_remote_copy(
            src_ref=outgoing.at[count + side], dst_ref=incoming.at[count + side],
            send_sem=edge_send.at[side], recv_sem=edge_recv.at[side],
            device_id=beside(side), device_id_type=MESH,
        )

    for c in range(chunks):
        start = c * CHUNK
        size = CHUNK if c < chunks - 1 else CHUNK + 2
        for n in range(size):
            source = place[start + n] if n < CHUNK else entries + n - CHUNK
            for kv in range(2):
                gathered[kv, n * tile : (n + 1) * tile, :] = blocks[source, kv]
        for part in range(width // wide):
            lanes = slice(part * wide, (part + 1) * wide)
            total_rows = dot(gathered[0, : size * tile], weights[2, lanes, :], NT)
            total_rows += dot(gathered[1, : size * tile], weights[3, lanes, :], NT)
            outgoing[start : start + size, :, lanes] = total_rows.astype(jnp.bfloat16).reshape(
                size, tile, wide
            )

        @pl.loop(1 if c == 0 else 0, CHUNK)
        def _(i):
            push(start + i, c).start()

    push_edge(0).start()
    push_edge(1).start()
    incoming[0] = outgoing[0]

    for part in range(width // wide):
        lanes = slice(part * wide, (part + 1) * wide)
        layer_ref[:, lanes] = dot(mixed[...], weights[1, :, lanes], NN).astype(jnp.bfloat16)
        total[:, lanes] = (
            dot(query_grad[...], weights[0, lanes, :], NT)
            + dot(sums[0], weights[2, lanes, :], NT)
            + dot(sums[1], weights[3, lanes, :], NT)
        )

    for c in range(chunks):
        some = pl.ds(1, CHUNK - 1) if c == 0 else pl.ds(c * CHUNK, CHUNK)
        pltpu.make_async_copy(incoming.at[some], incoming.at[some], recv_sem.at[c]).wait()
        start = c * CHUNK
        size = CHUNK
        if c == chunks - 1:
            push_edge(0).wait_recv()
            push_edge(1).wait_recv()
            size += 2
        for part in range(width // wide):
            lanes = slice(part * wide, (part + 1) * wide)
            came = incoming[start : start + size, :, lanes].reshape(size * tile, wide)
            whole = total[:, lanes] + dot(
                choose[:, start * tile : (start + size) * tile], came, NN
            )
            if c == chunks - 1:
                grad_ref[:, lanes] = whole.astype(jnp.bfloat16)
            else:
                total[:, lanes] = whole

    pltpu.make_async_copy(want_out.at[others], want_out.at[others], want_send).wait()
    pltpu.make_async_copy(rows_out.at[others], rows_out.at[others], row_send).wait()
    pltpu.make_async_copy(outgoing.at[others], outgoing.at[others], send_sem).wait()
    push_halo(0).wait_send()
    push_halo(1).wait_send()
    push_edge(0).wait_send()
    push_edge(1).wait_send()


def on_device(
    latents, w_query, w_key, w_value, w_out, cotangent, memory_ids, memory_count, tile_mask
):
    frames, tile, width = latents.shape
    count = lax.axis_size("tm")
    rows = latents.reshape(-1, width)
    mem = memory_ids.shape[1]
    inner = w_query.shape[1]
    head_dim = inner // HEADS
    cols = GROUP * head_dim
    steps = inner // cols
    own = frames * tile
    chunks = count // CHUNK

    vmem = pl.BlockSpec(memory_space=pltpu.VMEM)
    smem = pl.BlockSpec(memory_space=pltpu.SMEM)
    hbm = pl.BlockSpec(memory_space=pl.ANY)
    layer_out, latent_grad = pl.pallas_call(
        functools.partial(layer_kernel, count, frames, mem, tile, head_dim, steps),
        in_specs=[smem] * 3 + [vmem] + [hbm] * 5,
        out_specs=[vmem, vmem],
        out_shape=[
            jax.ShapeDtypeStruct((own, width), jnp.bfloat16),
            jax.ShapeDtypeStruct((own, width), jnp.bfloat16),
        ],
        scratch_shapes=[
            pltpu.VMEM((4, width, inner), jnp.bfloat16),
            pltpu.VMEM((own, width), jnp.bfloat16),
            pltpu.VMEM((own, inner), jnp.bfloat16),
            pltpu.VMEM((own, inner), jnp.bfloat16),
            pltpu.VMEM((own + 2 * tile, inner), jnp.bfloat16),
            pltpu.VMEM((own + 2 * tile, inner), jnp.bfloat16),
            pltpu.VMEM((count, tile, inner), jnp.bfloat16),
            pltpu.VMEM((count, tile, inner), jnp.bfloat16),
            pltpu.VMEM((count, 8, own), jnp.int32),
            pltpu.VMEM((count, 8, own), jnp.int32),
            pltpu.VMEM((own, (count + 2) * tile), jnp.bfloat16),
            pltpu.VMEM((count, tile, width), jnp.bfloat16),
            pltpu.VMEM((count + 2, tile, width), jnp.bfloat16),
            pltpu.VMEM((own, inner), jnp.bfloat16),
            pltpu.VMEM((own, inner), jnp.bfloat16),
            pltpu.VMEM((2, own, inner), jnp.bfloat16),
            pltpu.VMEM((frames * mem + 2, 2, tile, inner), jnp.bfloat16),
            pltpu.VMEM((2, (CHUNK + 2) * tile, inner), jnp.bfloat16),
            pltpu.VMEM((count + 2, tile, width), jnp.bfloat16),
            pltpu.VMEM((count + 2, tile, width), jnp.bfloat16),
            pltpu.VMEM((own, width), jnp.float32),
            pltpu.SMEM((frames * mem,), jnp.int32),
            pltpu.SMEM((count,), jnp.int32),
            pltpu.SemaphoreType.DMA((4,)),
            pltpu.SemaphoreType.DMA,
            pltpu.SemaphoreType.DMA,
            pltpu.SemaphoreType.DMA,
            pltpu.SemaphoreType.DMA,
            pltpu.SemaphoreType.DMA((chunks,)),
            pltpu.SemaphoreType.DMA((2,)),
            pltpu.SemaphoreType.DMA((2,)),
            pltpu.SemaphoreType.DMA,
            pltpu.SemaphoreType.DMA((chunks,)),
            pltpu.SemaphoreType.DMA((2,)),
            pltpu.SemaphoreType.DMA((2,)),
        ],
        compiler_params=pltpu.CompilerParams(
            collective_id=0, has_side_effects=True, vmem_limit_bytes=58 * 2**20
        ),
    )(
        memory_ids, memory_count, tile_mask.T, rows, cotangent.reshape(-1, width),
        w_query, w_out, w_key, w_value,
    )
    return (
        layer_out.reshape(frames, tile, width),
        latent_grad.reshape(frames, tile, width),
    )


def solution(mesh):
    placed = (
        P(("shard", "tm"), None, None),
        P(),
        P(),
        P(),
        P(),
        P(("shard", "tm"), None, None),
        P(("shard", "tm"), None),
        P(("shard", "tm")),
        P(("shard", "tm"), None),
    )
    return jax.shard_map(
        on_device,
        mesh=mesh,
        in_specs=placed,
        out_specs=(P(("shard", "tm"), None, None), P(("shard", "tm"), None, None)),
        check_vma=False,
    )
```

time: 128 us -> 99.5 us (0.78)
  Pallas kernels: 120 us -> 95.1 us
  other arithmetic: 1.95 us -> 0 us
  local copies, waits for them, and re-layouts: 5.04 us -> 3.53 us
    pallas_call x1, Pallas kernels: 120 us -> 95.1 us  [on_device(): pl.pallas_call(functools.partial(layer_kernel, count, frames, mem, tile,...]
    unnamed x3 -> x2, local copies, waits for them, and re-layouts: 4.87 us -> 3.53 us
where the time goes in v1:
time: 99.5 us; the launch traced here: 99.3 us
  Pallas kernels  95.1 us (96%)
  local copies, waits for them, and re-layouts  3.53 us (4%)
    pallas_call x1, Pallas kernels, on_device(): pl.pallas_call(functools.partial(layer_kernel, count, frames, mem, tile,...  95.1 us
    unnamed x2, local copies, waits for them, and re-layouts  3.53 us

profile of v1, /device:TPU:16, one launch (start us, length us, event | category | flops | bytes accessed | tf_op | source)
XLA Modules:
  0.0 99.3 jit_solution(17255796074373002858)
XLA Ops:
  0.6 95.1 %shard_map.104 = (bf16[128,1536]{1,0:T(8,128)(2,1)}, bf16[128,1536]{1,0:T(8,128)(2,1)}) custom-call(s32[4,4]{1,0:T(4,128)} %ids.1, s32[4]{0:T(128)} %recalled.1, s32[2,4]{1,0:T(2,128)} %bitcast.9, bf16[128,1536]{1,0:T(8,128)(2,1)} %bitcast.7, bf16[128,1536]{1,0:T(8,128)(2,1)} %bitcast.8, bf16[1536,1536]{1,0:T(8,128)(2,1)} %wq_hbm.1, ...), custom_call_target="tpu_custom_call" | custom-call | tf_op jit(solution)/shard_map/pallas_call | solution.py:386
  95.7 1.8 %copy.13 = bf16[4,32,1536]{2,1,0:T(8,128)(2,1)} copy(bf16[4,32,1536]{2,1,0:T(8,128)(2,1)} %bitcast.6) | data formatting | bytes 786432
  97.5 1.8 %copy.14 = bf16[4,32,1536]{2,1,0:T(8,128)(2,1)} copy(bf16[4,32,1536]{2,1,0:T(8,128)(2,1)} %bitcast.5) | data formatting | bytes 786432

commit v2 on v1

--- a/solution.py
+++ b/solution.py
@@ -26,17 +26,22 @@
     ids, recalled, tiles, x_ref, cot_hbm, wq_hbm, wo_hbm, wk_hbm, wv_hbm,
     layer_ref, grad_ref,
     weights, cot_ref, q_ref, g_ref, k_ext, v_ext, k_mem, v_mem, want_out, want_in, choose,
-    rows_out, rows_in, mixed, query_grad, sums, blocks, gathered, outgoing, incoming, total,
+    rows_out, rows_in, x_far, mixed, query_grad, sums, blocks, gathered, outgoing, incoming,
+    relay_out, relay_in, total,
     spots, place,
     weight_sem, cot_sem, want_send, want_recv, row_send, row_recv, halo_send, halo_recv,
-    send_sem, recv_sem, edge_send, edge_recv,
+    send_sem, recv_sem, edge_send, edge_recv, far_send, far_recv, relay_send, relay_recv,
 ):
     me = lax.axis_index("tm")
     width = x_ref.shape[1]
     own = x_ref.shape[0]
     cols = q_ref.shape[1] // steps
     wide = 2 * cols
+    half = count // 2
     chunks = count // CHUNK
+    near_chunks = half // CHUNK
+    place_in = lax.rem(me, half)
+    base = me - place_in
     entries = frames * mem
     scale = 1.0 / math.sqrt(head_dim)
     loads = [
@@ -49,15 +54,13 @@
     for load in loads[1:]:
         load.start()
 
-    def shift(i):
-        half = i // 2
-        return count // 2 + (i % 2) * 2 * half - half
-
-    def peer(i):
-        return {"tm": lax.rem(me + shift(i), count)}
+    def mate(i):
+        return {"tm": base + lax.rem(place_in + i, half)}
 
     def asker(i):
-        return {"tm": lax.rem(me + count - shift(i), count)}
+        return {"tm": base + lax.rem(place_in + half - i, half)}
+
+    partner = {"tm": lax.rem(me + half, count)}
 
     def beside(side):
         return {"tm": lax.rem(me + (1 if side == 0 else count - 1), count)}
@@ -66,17 +69,20 @@
 
     @pl.loop(1, count)
     def _(i):
-        pl.semaphore_signal(barrier, inc=1, device_id=peer(i), device_id_type=MESH)
+        pl.semaphore_signal(
+            barrier, inc=1, device_id={"tm": lax.rem(me + i, count)}, device_id_type=MESH
+        )
 
     slots = []
     slot_at = lax.broadcasted_iota(jnp.int32, want_out.shape, 0)
+    slot_at += half * lax.broadcasted_iota(jnp.int32, want_out.shape, 1)
     asked = jnp.full(want_out.shape, -frames, jnp.int32)
     for e in range(entries):
         frame = ids[e // mem, e % mem]
-        away = lax.rem(lax.div(frame, frames) - me + count, count)
-        slot = jnp.where(
-            away >= count // 2, 2 * away - count + 1, lax.rem(count - 2 * away, count)
-        )
+        owner = lax.div(frame, frames)
+        away = lax.rem(owner - place_in + count, half)
+        same = (owner >= base) & (owner < base + half)
+        slot = away + jnp.where(same, 0, half)
         spots[e] = slot
         slots.append(slot)
         asked = jnp.where(slot_at == slot, lax.rem(frame, frames), asked)
@@ -87,7 +93,7 @@
     def ask(i):
         return pltpu.make_async_remote_copy(
             src_ref=want_out.at[i], dst_ref=want_in.at[i], send_sem=want_send,
-            recv_sem=want_recv, device_id=peer(i), device_id_type=MESH,
+            recv_sem=want_recv, device_id=mate(i), device_id_type=MESH,
         )
 
     def push_halo(side):
@@ -98,48 +104,61 @@
             device_id=beside(side), device_id_type=MESH,
         )
 
+    swap = pltpu.make_async_remote_copy(
+        src_ref=x_ref, dst_ref=x_far, send_sem=far_send, recv_sem=far_recv,
+        device_id=partner, device_id_type=MESH,
+    )
+
     def push_row(i, c):
         return pltpu.make_async_remote_copy(
             src_ref=rows_out.at[i], dst_ref=rows_in.at[i], send_sem=row_send,
-            recv_sem=row_recv.at[c], device_id=asker(i), device_id_type=MESH,
-        )
-
-    @pl.loop(1, count)
+            recv_sem=row_recv.at[c], device_id=asker(lax.rem(i, half)), device_id_type=MESH,
+        )
+
+    def remote_slots(c):
+        start = c * CHUNK
+        return start + (1 if start % half == 0 else 0), start + CHUNK
+
+    @pl.loop(1, half)
     def _(i):
         ask(i).start()
 
+    swap.start()
     push_halo(0).start()
     push_halo(1).start()
     want_in[0] = want_out[0]
-    others = pl.ds(1, count - 1)
-    pltpu.make_async_copy(want_in.at[others], want_in.at[others], want_recv).wait()
+    mates = pl.ds(1, half - 1)
+    pltpu.make_async_copy(want_in.at[mates], want_in.at[mates], want_recv).wait()
 
     shape = (CHUNK, tile, own)
     token = lax.broadcasted_iota(jnp.int32, shape, 1)
     lane = lax.broadcasted_iota(jnp.int32, shape, 2)
 
     def pick_rows(c):
-        asked = want_in[pl.ds(c * CHUNK, CHUNK)][:, 0:1, :]
+        some = pl.ds(c * CHUNK, CHUNK)
+        far = c // near_chunks
+        asked = want_in[c % near_chunks * CHUNK : (c % near_chunks + 1) * CHUNK, far, 0:1, :]
         hot = jnp.where(lane == asked * tile + token, 1.0, 0.0).reshape(CHUNK * tile, own)
         low = hot.astype(jnp.bfloat16)
+        source = x_far if far else x_ref
         for part in range(width // wide):
             lanes = slice(part * wide, (part + 1) * wide)
-            rows_out[pl.ds(c * CHUNK, CHUNK), :, lanes] = (
-                dot(low, x_ref[:, lanes], NN).astype(jnp.bfloat16).reshape(CHUNK, tile, wide)
+            rows_out[some, :, lanes] = (
+                dot(low, source[:, lanes], NN).astype(jnp.bfloat16).reshape(CHUNK, tile, wide)
             )
-        return hot
-
-    hots = []
-    for c in range(chunks):
-        hots.append(pick_rows(c))
-
-        @pl.loop(1 if c == 0 else 0, CHUNK)
+        start, stop = remote_slots(c)
+
+        @pl.loop(start, stop)
         def _(i):
-            push_row(c * CHUNK + i, c).start()
-
-    rows_in[0] = rows_out[0]
-    for c in range(chunks):
-        choose[:, c * CHUNK * tile : (c + 1) * CHUNK * tile] = hots[c].T.astype(jnp.bfloat16)
+            push_row(i, c).start()
+
+        if start != c * CHUNK:
+            rows_in[c * CHUNK] = rows_out[c * CHUNK]
+        choose[:, c * CHUNK * tile : (c + 1) * CHUNK * tile] = hot.T.astype(jnp.bfloat16)
+
+    for c in range(near_chunks):
+        pick_rows(c)
+
     edge_row = lax.broadcasted_iota(jnp.int32, (own, 2 * tile), 0)
     edge_lane = lax.broadcasted_iota(jnp.int32, (own, 2 * tile), 1)
     edge_spot = jnp.where(edge_lane < tile, edge_lane, edge_lane + (frames - 2) * tile)
@@ -181,6 +200,9 @@
         v_ext[:, lanes] = dot(ext, weights[3, :, lanes], NN).astype(jnp.bfloat16)
 
     def project(c):
+        start, stop = remote_slots(c)
+        came = pl.ds(start, stop - start)
+        pltpu.make_async_copy(rows_in.at[came], rows_in.at[came], row_recv.at[c]).wait()
         some = pl.ds(c * CHUNK, CHUNK)
 
         @pl.loop(0, width // wide)
@@ -194,14 +216,10 @@
                     .reshape(CHUNK, tile, wide)
                 )
 
-    first = pl.ds(1, CHUNK - 1)
-    pltpu.make_async_copy(rows_in.at[first], rows_in.at[first], row_recv.at[0]).wait()
-    project(0)
-
-    @pl.loop(1, chunks)
-    def _(c):
-        some = pl.ds(c * CHUNK, CHUNK)
-        pltpu.make_async_copy(rows_in.at[some], rows_in.at[some], row_recv.at[c]).wait()
+    swap.wait_recv()
+    for c in range(near_chunks, chunks):
+        pick_rows(c)
+    for c in range(chunks):
         project(c)
 
     rows = GROUP * tile
@@ -295,8 +313,13 @@
     def push(i, c):
         return pltpu.make_async_remote_copy(
             src_ref=outgoing.at[i], dst_ref=incoming.at[i], send_sem=send_sem,
-            recv_sem=recv_sem.at[c], device_id=peer(i), device_id_type=MESH,
-        )
+            recv_sem=recv_sem.at[c], device_id=mate(lax.rem(i, half)), device_id_type=MESH,
+        )
+
+    relay = pltpu.make_async_remote_copy(
+        src_ref=relay_out, dst_ref=relay_in, send_sem=relay_send, recv_sem=relay_recv,
+        device_id=partner, device_id_type=MESH,
+    )
 
     def push_edge(side):
         return pltpu.make_async_remote_copy(
@@ -305,28 +328,48 @@
             device_id=beside(side), device_id_type=MESH,
         )
 
-    for c in range(chunks):
+    for c in list(range(near_chunks, chunks)) + list(range(near_chunks)):
         start = c * CHUNK
-        size = CHUNK if c < chunks - 1 else CHUNK + 2
-        for n in range(size):
+        extra = 2 if c == near_chunks - 1 else 0
+        for n in range(CHUNK + extra):
             source = place[start + n] if n < CHUNK else entries + n - CHUNK
             for kv in range(2):
                 gathered[kv, n * tile : (n + 1) * tile, :] = blocks[source, kv]
+        taken = (CHUNK + extra) * tile
         for part in range(width // wide):
             lanes = slice(part * wide, (part + 1) * wide)
-            total_rows = dot(gathered[0, : size * tile], weights[2, lanes, :], NT)
-            total_rows += dot(gathered[1, : size * tile], weights[3, lanes, :], NT)
-            outgoing[start : start + size, :, lanes] = total_rows.astype(jnp.bfloat16).reshape(
-                size, tile, wide
-            )
-
-        @pl.loop(1 if c == 0 else 0, CHUNK)
+            sent = dot(gathered[0, :taken], weights[2, lanes, :], NT)
+            sent += dot(gathered[1, :taken], weights[3, lanes, :], NT)
+            sent = sent.astype(jnp.bfloat16).reshape(CHUNK + extra, tile, wide)
+            outgoing[start : start + CHUNK, :, lanes] = sent[:CHUNK]
+            if extra:
+                outgoing[count : count + 2, :, lanes] = sent[CHUNK:]
+        first, stop = remote_slots(c)
+
+        @pl.loop(first, stop)
         def _(i):
-            push(start + i, c).start()
+            push(i, c).start()
+
+        if first != start:
+            incoming[start] = outgoing[start]
 
     push_edge(0).start()
     push_edge(1).start()
-    incoming[0] = outgoing[0]
+
+    def await_chunk(c):
+        start, stop = remote_slots(c)
+        came = pl.ds(start, stop - start)
+        pltpu.make_async_copy(incoming.at[came], incoming.at[came], recv_sem.at[c]).wait()
+
+    for c in range(near_chunks, chunks):
+        await_chunk(c)
+    for part in range(width // wide):
+        lanes = slice(part * wide, (part + 1) * wide)
+        came = incoming[half:count, :, lanes].reshape(half * tile, wide)
+        relay_out[:, lanes] = dot(choose[:, half * tile : count * tile], came, NN).astype(
+            jnp.bfloat16
+        )
+    relay.start()
 
     for part in range(width // wide):
         lanes = slice(part * wide, (part + 1) * wide)
@@ -337,29 +380,26 @@
             + dot(sums[1], weights[3, lanes, :], NT)
         )
 
-    for c in range(chunks):
-        some = pl.ds(1, CHUNK - 1) if c == 0 else pl.ds(c * CHUNK, CHUNK)
-        pltpu.make_async_copy(incoming.at[some], incoming.at[some], recv_sem.at[c]).wait()
-        start = c * CHUNK
-        size = CHUNK
-        if c == chunks - 1:
-            push_edge(0).wait_recv()
-            push_edge(1).wait_recv()
-            size += 2
-        for part in range(width // wide):
-            lanes = slice(part * wide, (part + 1) * wide)
-            came = incoming[start : start + size, :, lanes].reshape(size * tile, wide)
-            whole = total[:, lanes] + dot(
-                choose[:, start * tile : (start + size) * tile], came, NN
-            )
-            if c == chunks - 1:
-                grad_ref[:, lanes] = whole.astype(jnp.bfloat16)
-            else:
-                total[:, lanes] = whole
-
-    pltpu.make_async_copy(want_out.at[others], want_out.at[others], want_send).wait()
-    pltpu.make_async_copy(rows_out.at[others], rows_out.at[others], row_send).wait()
-    pltpu.make_async_copy(outgoing.at[others], outgoing.at[others], send_sem).wait()
+    for c in range(near_chunks):
+        await_chunk(c)
+    push_edge(0).wait_recv()
+    push_edge(1).wait_recv()
+    for part in range(width // wide):
+        lanes = slice(part * wide, (part + 1) * wide)
+        came = incoming[0:half, :, lanes].reshape(half * tile, wide)
+        edges = incoming[count : count + 2, :, lanes].reshape(2 * tile, wide)
+        total[:, lanes] += dot(choose[:, : half * tile], came, NN) + dot(
+            choose[:, count * tile :], edges, NN
+        )
+    relay.wait_recv()
+    grad_ref[...] = (total[...] + relay_in[...].astype(jnp.float32)).astype(jnp.bfloat16)
+
+    pltpu.make_async_copy(want_out.at[mates], want_out.at[mates], want_send).wait()
+    sent_rows = pl.ds(0, count - 2)
+    pltpu.make_async_copy(rows_out.at[sent_rows], rows_out.at[sent_rows], row_send).wait()
+    pltpu.make_async_copy(outgoing.at[sent_rows], outgoing.at[sent_rows], send_sem).wait()
+    swap.wait_send()
+    relay.wait_send()
     push_halo(0).wait_send()
     push_halo(1).wait_send()
     push_edge(0).wait_send()
@@ -400,11 +440,12 @@
             pltpu.VMEM((own + 2 * tile, inner), jnp.bfloat16),
             pltpu.VMEM((count, tile, inner), jnp.bfloat16),
             pltpu.VMEM((count, tile, inner), jnp.bfloat16),
-            pltpu.VMEM((count, 8, own), jnp.int32),
-            pltpu.VMEM((count, 8, own), jnp.int32),
+            pltpu.VMEM((count // 2, 2, 8, own), jnp.int32),
+            pltpu.VMEM((count // 2, 2, 8, own), jnp.int32),
             pltpu.VMEM((own, (count + 2) * tile), jnp.bfloat16),
             pltpu.VMEM((count, tile, width), jnp.bfloat16),
             pltpu.VMEM((count + 2, tile, width), jnp.bfloat16),
+            pltpu.VMEM((own, width), jnp.bfloat16),
             pltpu.VMEM((own, inner), jnp.bfloat16),
             pltpu.VMEM((own, inner), jnp.bfloat16),
             pltpu.VMEM((2, own, inner), jnp.bfloat16),
@@ -412,6 +453,8 @@
             pltpu.VMEM((2, (CHUNK + 2) * tile, inner), jnp.bfloat16),
             pltpu.VMEM((count + 2, tile, width), jnp.bfloat16),
             pltpu.VMEM((count + 2, tile, width), jnp.bfloat16),
+            pltpu.VMEM((own, width), jnp.bfloat16),
+            pltpu.VMEM((own, width), jnp.bfloat16),
             pltpu.VMEM((own, width), jnp.float32),
             pltpu.SMEM((frames * mem,), jnp.int32),
             pltpu.SMEM((count,), jnp.int32),
@@ -427,6 +470,10 @@
             pltpu.SemaphoreType.DMA((chunks,)),
             pltpu.SemaphoreType.DMA((2,)),
             pltpu.SemaphoreType.DMA((2,)),
+            pltpu.SemaphoreType.DMA,
+            pltpu.SemaphoreType.DMA,
+            pltpu.SemaphoreType.DMA,
+            pltpu.SemaphoreType.DMA,
         ],
         compiler_params=pltpu.CompilerParams(
             collective_id=0, has_side_effects=True, vmem_limit_bytes=58 * 2**20

time: 99.5 us -> 87.5 us (0.88); the launches traced: 99.3 us -> 85.9 us
  Pallas kernels: 95.1 us -> 81.7 us
    pallas_call x1, Pallas kernels: 95.1 us -> 81.7 us  [on_device(): pl.pallas_call(functools.partial(layer_kernel, count, frames, mem, tile,...]
where the time goes in v2:
time: 87.5 us; the launch traced here: 85.9 us
  Pallas kernels  81.7 us (93%)
  local copies, waits for them, and re-layouts  3.53 us (4%)
    pallas_call x1, Pallas kernels, on_device(): pl.pallas_call(functools.partial(layer_kernel, count, frames, mem, tile,...  81.7 us
    unnamed x2, local copies, waits for them, and re-layouts  3.53 us

profile of v2, /device:TPU:16, one launch (start us, length us, event | category | flops | bytes accessed | tf_op | source)
XLA Modules:
  0.0 85.9 jit_solution(17996467613508328850)
XLA Ops:
  0.6 81.7 %shard_map.104 = (bf16[128,1536]{1,0:T(8,128)(2,1)}, bf16[128,1536]{1,0:T(8,128)(2,1)}) custom-call(s32[4,4]{1,0:T(4,128)} %ids.1, s32[4]{0:T(128)} %recalled.1, s32[2,4]{1,0:T(2,128)} %bitcast.9, bf16[128,1536]{1,0:T(8,128)(2,1)} %bitcast.7, bf16[128,1536]{1,0:T(8,128)(2,1)} %bitcast.8, bf16[1536,1536]{1,0:T(8,128)(2,1)} %wq_hbm.1, ...), custom_call_target="tpu_custom_call" | custom-call | tf_op jit(solution)/shard_map/pallas_call | solution.py:426
  82.4 1.8 %copy.13 = bf16[4,32,1536]{2,1,0:T(8,128)(2,1)} copy(bf16[4,32,1536]{2,1,0:T(8,128)(2,1)} %bitcast.6) | data formatting | bytes 786432
  84.1 1.8 %copy.14 = bf16[4,32,1536]{2,1,0:T(8,128)(2,1)} copy(bf16[4,32,1536]{2,1,0:T(8,128)(2,1)} %bitcast.5) | data formatting | bytes 786432

commit v3 on v2

v3 whole, which is shorter than its diff:
```python
import functools
import math

import jax
import jax.numpy as jnp
from jax import lax
from jax.experimental import pallas as pl
from jax.experimental.pallas import tpu as pltpu
from jax.sharding import PartitionSpec as P

HEADS = 24
GROUP = 4
NT = (((1,), (1,)), ((), ()))
NN = (((1,), (0,)), ((), ()))
TN = (((0,), (0,)), ((), ()))
MESH = pl.DeviceIdType.MESH


def dot(a, b, dims):
    return lax.dot_general(a, b, dims, preferred_element_type=jnp.float32)


def layer_kernel(
    count, frames, mem, tile, head_dim, steps,
    ids, recalled, tiles, x_ref, cot_hbm, wq_hbm, wo_hbm, wk_hbm, wv_hbm,
    layer_ref, grad_ref,
    weights, cot_ref, q_ref, g_ref, k_ext, v_ext, k_mem, v_mem, want_out, want_in, choose,
    rows_out, rows_in, far_out, far_in, x_far, far_sum, kept, mixed, query_grad, sums, blocks,
    gathered, near_in, back_in, relay_out, relay_in, total,
    spots, place,
    weight_sem, cot_sem, want_send, want_recv, row_send, row_recv, far_send, far_recv,
    halo_send, halo_recv, near_send, near_recv, back_send, back_recv, edge_send, edge_recv,
    swap_send, swap_recv, relay_send, relay_recv,
):
    me = lax.axis_index("tm")
    width = x_ref.shape[1]
    own = x_ref.shape[0]
    cols = q_ref.shape[1] // steps
    wide = 2 * cols
    half = count // 2
    pieces = width // wide
    cuts = [slice(p * wide, (p + 1) * wide) for p in range(pieces)]
    place_in = lax.rem(me, half)
    base = me - place_in
    entries = frames * mem
    scale = 1.0 / math.sqrt(head_dim)
    loads = [
        pltpu.make_async_copy(source, weights.at[i], weight_sem.at[i])
        for i, source in enumerate((wq_hbm, wo_hbm, wk_hbm, wv_hbm))
    ]
    load_cot = pltpu.make_async_copy(cot_hbm, cot_ref, cot_sem)
    loads[0].start()
    load_cot.start()
    for load in loads[1:]:
        load.start()

    def mate(i):
        return {"tm": base + lax.rem(place_in + i, half)}

    def asker(i):
        return {"tm": base + lax.rem(place_in + half - i, half)}

    partner = {"tm": lax.rem(me + half, count)}

    def beside(side):
        return {"tm": lax.rem(me + (1 if side == 0 else count - 1), count)}

    barrier = pltpu.get_barrier_semaphore()

    @pl.loop(1, count)
    def _(i):
        pl.semaphore_signal(
            barrier, inc=1, device_id={"tm": lax.rem(me + i, count)}, device_id_type=MESH
        )

    slots = []
    slot_at = lax.broadcasted_iota(jnp.int32, want_out.shape, 0)
    slot_at += half * lax.broadcasted_iota(jnp.int32, want_out.shape, 1)
    asked = jnp.full(want_out.shape, -frames, jnp.int32)
    for e in range(entries):
        frame = ids[e // mem, e % mem]
        owner = lax.div(frame, frames)
        away = lax.rem(owner - place_in + count, half)
        same = (owner >= base) & (owner < base + half)
        slot = away + jnp.where(same, 0, half)
        spots[e] = slot
        slots.append(slot)
        asked = jnp.where(slot_at == slot, lax.rem(frame, frames), asked)
    want_out[...] = asked

    pl.semaphore_wait(barrier, count - 1)

    def ask(i):
        return pltpu.make_async_remote_copy(
            src_ref=want_out.at[i], dst_ref=want_in.at[i], send_sem=want_send,
            recv_sem=want_recv, device_id=mate(i), device_id_type=MESH,
        )

    def push_halo(side):
        return pltpu.make_async_remote_copy(
            src_ref=x_ref.at[pl.ds((frames - 1) * tile if side == 0 else 0, tile)],
            dst_ref=rows_in.at[half + side],
            send_sem=halo_send.at[side], recv_sem=halo_recv.at[side],
            device_id=beside(side), device_id_type=MESH,
        )

    def swap(p):
        return pltpu.make_async_remote_copy(
            src_ref=x_ref.at[:, cuts[p]], dst_ref=x_far.at[:, cuts[p]],
            send_sem=swap_send.at[p], recv_sem=swap_recv.at[p],
            device_id=partner, device_id_type=MESH,
        )

    def push_row(i):
        return pltpu.make_async_remote_copy(
            src_ref=rows_out.at[i], dst_ref=rows_in.at[i], send_sem=row_send,
            recv_sem=row_recv, device_id=asker(i), device_id_type=MESH,
        )

    def push_far(p, i):
        return pltpu.make_async_remote_copy(
            src_ref=far_out.at[p, i], dst_ref=far_in.at[p, i], send_sem=far_send.at[p],
            recv_sem=far_recv.at[p], device_id=asker(i), device_id_type=MESH,
        )

    @pl.loop(1, half)
    def _(i):
        ask(i).start()

    for p in range(pieces):
        swap(p).start()
    push_halo(0).start()
    push_halo(1).start()
    want_in[0] = want_out[0]
    mates = pl.ds(1, half - 1)
    pltpu.make_async_copy(want_in.at[mates], want_in.at[mates], want_recv).wait()

    shape = (half, tile, own)
    token = lax.broadcasted_iota(jnp.int32, shape, 1)
    lane = lax.broadcasted_iota(jnp.int32, shape, 2)

    def hot(far):
        picked = lane == want_in[:, far, 0:1, :] * tile + token
        return jnp.where(picked, 1.0, 0.0).reshape(half * tile, own)

    near_hot = hot(0).astype(jnp.bfloat16)
    for p in range(pieces):
        rows_out[0:half, :, cuts[p]] = (
            dot(near_hot, x_ref[:, cuts[p]], NN).astype(jnp.bfloat16).reshape(half, tile, wide)
        )

    @pl.loop(1, half)
    def _(i):
        push_row(i).start()

    rows_in[0] = rows_out[0]

    def pick_far(p):
        far_hot = hot(1).astype(jnp.bfloat16)
        swap(p).wait_recv()
        far_out[p] = (
            dot(far_hot, x_far[:, cuts[p]], NN).astype(jnp.bfloat16).reshape(half, tile, wide)
        )

        @pl.loop(1, half)
        def _(i):
            push_far(p, i).start()

        far_in[p, 0] = far_out[p, 0]

    choose[:, : half * tile] = hot(0).T.astype(jnp.bfloat16)
    choose[:, half * tile : count * tile] = hot(1).T.astype(jnp.bfloat16)
    edge_row = lax.broadcasted_iota(jnp.int32, (own, 2 * tile), 0)
    edge_lane = lax.broadcasted_iota(jnp.int32, (own, 2 * tile), 1)
    edge_spot = jnp.where(edge_lane < tile, edge_lane, edge_lane + (frames - 2) * tile)
    choose[:, count * tile : (count + 2) * tile] = jnp.where(
        edge_row == edge_spot, 1.0, 0.0
    ).astype(jnp.bfloat16)

    for i in range(count):
        at = jnp.int32(0)
        for e in range(entries):
            at = jnp.where(slots[e] == i, e, at)
        place[i] = at

    loads[0].wait()

    @pl.loop(0, pieces)
    def _(p):
        lanes = pl.ds(pl.multiple_of(p * wide, wide), wide)
        q_ref[:, lanes] = dot(x_ref[...], weights[0, :, lanes], NN).astype(jnp.bfloat16)

    pick_far(0)
    load_cot.wait()
    loads[1].wait()

    @pl.loop(0, pieces)
    def _(p):
        lanes = pl.ds(pl.multiple_of(p * wide, wide), wide)
        g_ref[:, lanes] = dot(cot_ref[...], weights[1, lanes, :], NT).astype(jnp.bfloat16)

    push_halo(0).wait_recv()
    push_halo(1).wait_recv()
    loads[2].wait()
    loads[3].wait()

    @pl.loop(0, pieces)
    def _(p):
        lanes = pl.ds(pl.multiple_of(p * wide, wide), wide)
        ext = jnp.concatenate([rows_in[half], x_ref[...], rows_in[half + 1]], axis=0)
        k_ext[:, lanes] = dot(ext, weights[2, :, lanes], NN).astype(jnp.bfloat16)
        v_ext[:, lanes] = dot(ext, weights[3, :, lanes], NN).astype(jnp.bfloat16)

    for p in range(1, pieces):
        pick_far(p)

    mates_rows = rows_in.at[mates]
    pltpu.make_async_copy(mates_rows, mates_rows, row_recv).wait()

    @pl.loop(0, pieces)
    def _(p):
        lanes = pl.ds(pl.multiple_of(p * wide, wide), wide)
        flat = rows_in[0:half].reshape(half * tile, width)
        for weight, mem_ref in ((2, k_mem), (3, v_mem)):
            mem_ref[0:half, :, lanes] = (
                dot(flat, weights[weight, :, lanes], NN)
                .astype(jnp.bfloat16)
                .reshape(half, tile, wide)
            )

    for piece in range(pieces):
        came = far_in.at[piece, mates]
        pltpu.make_async_copy(came, came, far_recv.at[piece]).wait()

        @pl.loop(0, pieces)
        def _(p):
            lanes = pl.ds(pl.multiple_of(p * wide, wide), wide)
            flat = far_in[piece].reshape(half * tile, wide)
            for kv, mem_ref in enumerate((k_mem, v_mem)):
                part = dot(flat, weights[2 + kv, cuts[piece], lanes], NN)
                if piece > 0:
                    part += far_sum[kv, :, lanes]
                if piece < pieces - 1:
                    far_sum[kv, :, lanes] = part
                else:
                    mem_ref[half:count, :, lanes] = part.astype(jnp.bfloat16).reshape(
                        half, tile, wide
                    )

    rows = GROUP * tile
    own_head = (
        lax.broadcasted_iota(jnp.int32, (rows, cols), 0) // tile
        == lax.broadcasted_iota(jnp.int32, (rows, cols), 1) // head_dim
    )
    head_at = lax.broadcasted_iota(jnp.int32, (tile, cols), 1) // head_dim

    def spread(block):
        tall = jnp.concatenate([block] * GROUP, axis=0)
        return jnp.where(own_head, tall, jnp.zeros_like(tall))

    def fold(tall):
        flat = tall[0:tile]
        for part in range(1, GROUP):
            flat = jnp.where(head_at == part, tall[part * tile : (part + 1) * tile], flat)
        return flat

    def hide(f):
        frame = me * frames + f
        lower = (frame >= 1) & (tiles[0, f] == 1)
        upper = (frame < frames * count - 1) & (tiles[1, f] == 1)
        kept = [lower, None, upper] + [recalled[f] > j for j in range(mem)]
        return [None if k is None else jnp.where(k, 0.0, -1e30) for k in kept]

    def gather(f, lanes, ext, far):
        near = slice(f * tile, (f + 3) * tile)
        return jnp.concatenate(
            [ext[near, lanes]] + [far[spots[f * mem + j], :, lanes] for j in range(mem)],
            axis=0,
        )

    def attend(g):
        lanes = pl.ds(pl.multiple_of(g * cols, cols), cols)
        kept_at = pl.ds(pl.multiple_of(g * rows, rows), rows)
        held = [None, None]
        late = [None, None]
        for f in range(frames):
            here = slice(f * tile, (f + 1) * tile)
            keys = gather(f, lanes, k_ext, k_mem)
            values = gather(f, lanes, v_ext, v_mem)
            queries = spread(q_ref[here, lanes] * scale)
            grads = spread(g_ref[here, lanes])
            scores = dot(keys, queries, NT)
            scores = jnp.concatenate(
                [
                    part if bias is None else part + bias
                    for bias, part in zip(hide(f), jnp.split(scores, 3 + mem, axis=0))
                ],
                axis=0,
            )
            expo = jnp.exp(scores - jnp.max(scores, axis=0, keepdims=True))
            prob = expo * (1.0 / jnp.sum(expo, axis=0, keepdims=True))
            low = prob.astype(jnp.bfloat16)
            prob_grad = dot(values, grads, NT)
            delta = jnp.sum(prob * prob_grad, axis=0, keepdims=True)
            score_grad = (prob * (prob_grad - delta)).astype(jnp.bfloat16)
            kept[0, f, :, kept_at] = low
            kept[1, f, :, kept_at] = score_grad
            parts = (
                dot(score_grad, queries, NN).astype(jnp.bfloat16),
                dot(low, grads, NN).astype(jnp.bfloat16),
            )
            for kv, part in enumerate(parts):
                before = part[0:tile]
                middle = part[tile : 2 * tile].astype(jnp.float32)
                after = part[2 * tile : 3 * tile]
                if f == 0:
                    blocks[entries + 1, kv, :, lanes] = before
                else:
                    back = slice((f - 1) * tile, f * tile)
                    sums[kv, back, lanes] = (held[kv] + before.astype(jnp.float32)).astype(
                        jnp.bfloat16
                    )
                    middle = middle + late[kv]
                if f == frames - 1:
                    blocks[entries, kv, :, lanes] = after
                    sums[kv, here, lanes] = middle.astype(jnp.bfloat16)
                held[kv] = middle
                late[kv] = after.astype(jnp.float32)
                for j in range(mem):
                    blocks[f * mem + j, kv, :, lanes] = part[(3 + j) * tile : (4 + j) * tile]

    @pl.loop(0, steps)
    def _(g):
        attend(g)

    def finish(g):
        lanes = pl.ds(pl.multiple_of(g * cols, cols), cols)
        kept_at = pl.ds(pl.multiple_of(g * rows, rows), rows)
        for f in range(frames):
            here = slice(f * tile, (f + 1) * tile)
            keys = gather(f, lanes, k_ext, k_mem)
            values = gather(f, lanes, v_ext, v_mem)
            mixed[here, lanes] = fold(dot(kept[0, f, :, kept_at], values, TN)).astype(
                jnp.bfloat16
            )
            query_grad[here, lanes] = (
                fold(dot(kept[1, f, :, kept_at], keys, TN)) * scale
            ).astype(jnp.bfloat16)

    def push_near(i):
        return pltpu.make_async_remote_copy(
            src_ref=rows_out.at[i], dst_ref=near_in.at[i], send_sem=near_send,
            recv_sem=near_recv, device_id=mate(i), device_id_type=MESH,
        )

    def push_back(p, i):
        return pltpu.make_async_remote_copy(
            src_ref=far_out.at[p, i], dst_ref=back_in.at[p, i], send_sem=back_send.at[p],
            recv_sem=back_recv.at[p], device_id=mate(i), device_id_type=MESH,
        )

    def relay(p):
        return pltpu.make_async_remote_copy(
            src_ref=relay_out.at[p], dst_ref=relay_in.at[p], send_sem=relay_send.at[p],
            recv_sem=relay_recv.at[p], device_id=partner, device_id_type=MESH,
        )

    def push_edge(side):
        return pltpu.make_async_remote_copy(
            src_ref=rows_out.at[half + side], dst_ref=near_in.at[half + side],
            send_sem=edge_send.at[side], recv_sem=edge_recv.at[side],
            device_id=beside(side), device_id_type=MESH,
        )

    def collect(start, extra):
        for n in range(half + extra):
            source = place[start + n] if n < half else entries + n - half
            for kv in range(2):
                gathered[kv, n * tile : (n + 1) * tile, :] = blocks[source, kv]

    def weigh(p, slots_here):
        taken = slots_here * tile
        sent = dot(gathered[0, :taken], weights[2, cuts[p], :], NT)
        sent += dot(gathered[1, :taken], weights[3, cuts[p], :], NT)
        return sent.astype(jnp.bfloat16).reshape(slots_here, tile, wide)

    collect(half, 0)
    for p in range(pieces):
        gone = far_out.at[p, mates]
        pltpu.make_async_copy(gone, gone, far_send.at[p]).wait()
        far_out[p] = weigh(p, half)

        @pl.loop(1, half)
        def _(i):
            push_back(p, i).start()

        back_in[p, 0] = far_out[p, 0]

    collect(0, 2)
    gone = rows_out.at[mates]
    pltpu.make_async_copy(gone, gone, row_send).wait()
    for p in range(pieces):
        rows_out[:, :, cuts[p]] = weigh(p, half + 2)

    for p in range(pieces):
        came = back_in.at[p, mates]
        pltpu.make_async_copy(came, came, back_recv.at[p]).wait()
        relay_out[p] = dot(
            choose[:, half * tile : count * tile], back_in[p].reshape(half * tile, wide), NN
        ).astype(jnp.bfloat16)
        relay(p).start()
        if p == 0:

            @pl.loop(1, half)
            def _(i):
                push_near(i).start()

            push_edge(0).start()
            push_edge(1).start()
            near_in[0] = rows_out[0]

    @pl.loop(0, steps)
    def _(g):
        finish(g)

    for p in range(pieces):
        lanes = cuts[p]
        layer_ref[:, lanes] = dot(mixed[...], weights[1, :, lanes], NN).astype(jnp.bfloat16)
        total[:, lanes] = (
            dot(query_grad[...], weights[0, lanes, :], NT)
            + dot(sums[0], weights[2, lanes, :], NT)
            + dot(sums[1], weights[3, lanes, :], NT)
        )

    came = near_in.at[mates]
    pltpu.make_async_copy(came, came, near_recv).wait()
    push_edge(0).wait_recv()
    push_edge(1).wait_recv()
    for p in range(pieces):
        lanes = cuts[p]
        total[:, lanes] += dot(
            choose[:, : half * tile], near_in[0:half, :, lanes].reshape(half * tile, wide), NN
        ) + dot(
            choose[:, count * tile :],
            near_in[half : half + 2, :, lanes].reshape(2 * tile, wide),
            NN,
        )
    for p in range(pieces):
        relay(p).wait_recv()
        grad_ref[:, cuts[p]] = (total[:, cuts[p]] + relay_in[p].astype(jnp.float32)).astype(
            jnp.bfloat16
        )

    asked_of = want_out.at[mates]
    pltpu.make_async_copy(asked_of, asked_of, want_send).wait()
    gone = rows_out.at[mates]
    pltpu.make_async_copy(gone, gone, near_send).wait()
    for p in range(pieces):
        gone = far_out.at[p, mates]
        pltpu.make_async_copy(gone, gone, back_send.at[p]).wait()
        swap(p).wait_send()
        relay(p).wait_send()
    push_halo(0).wait_send()
    push_halo(1).wait_send()
    push_edge(0).wait_send()
    push_edge(1).wait_send()


def hand_over(layer_in, grad_in, layer_ref, grad_ref):
    layer_ref[...] = layer_in[...]
    grad_ref[...] = grad_in[...]


def on_device(
    latents, w_query, w_key, w_value, w_out, cotangent, memory_ids, memory_count, tile_mask
):
    frames, tile, width = latents.shape
    count = lax.axis_size("tm")
    rows = latents.reshape(-1, width)
    mem = memory_ids.shape[1]
    inner = w_query.shape[1]
    head_dim = inner // HEADS
    cols = GROUP * head_dim
    steps = inner // cols
    own = frames * tile
    half = count // 2
    wide = 2 * cols
    pieces = width // wide

    vmem = pl.BlockSpec(memory_space=pltpu.VMEM)
    smem = pl.BlockSpec(memory_space=pltpu.SMEM)
    hbm = pl.BlockSpec(memory_space=pl.ANY)
    layer_out, latent_grad = pl.pallas_call(
        functools.partial(layer_kernel, count, frames, mem, tile, head_dim, steps),
        in_specs=[smem] * 3 + [vmem] + [hbm] * 5,
        out_specs=[vmem, vmem],
        out_shape=[
            jax.ShapeDtypeStruct((own, width), jnp.bfloat16),
            jax.ShapeDtypeStruct((own, width), jnp.bfloat16),
        ],
        scratch_shapes=[
            pltpu.VMEM((4, width, inner), jnp.bfloat16),
            pltpu.VMEM((own, width), jnp.bfloat16),
            pltpu.VMEM((own, inner), jnp.bfloat16),
            pltpu.VMEM((own, inner), jnp.bfloat16),
            pltpu.VMEM((own + 2 * tile, inner), jnp.bfloat16),
            pltpu.VMEM((own + 2 * tile, inner), jnp.bfloat16),
            pltpu.VMEM((count, tile, inner), jnp.bfloat16),
            pltpu.VMEM((count, tile, inner), jnp.bfloat16),
            pltpu.VMEM((half, 2, 8, own), jnp.int32),
            pltpu.VMEM((half, 2, 8, own), jnp.int32),
            pltpu.VMEM((own, (count + 2) * tile), jnp.bfloat16),
            pltpu.VMEM((half + 2, tile, width), jnp.bfloat16),
            pltpu.VMEM((half + 2, tile, width), jnp.bfloat16),
            pltpu.VMEM((pieces, half, tile, wide), jnp.bfloat16),
            pltpu.VMEM((pieces, half, tile, wide), jnp.bfloat16),
            pltpu.VMEM((own, width), jnp.bfloat16),
            pltpu.VMEM((2, half * tile, inner), jnp.float32),
            pltpu.VMEM((2, frames, (3 + mem) * tile, steps * GROUP * tile), jnp.bfloat16),
            pltpu.VMEM((own, inner), jnp.bfloat16),
            pltpu.VMEM((own, inner), jnp.bfloat16),
            pltpu.VMEM((2, own, inner), jnp.bfloat16),
            pltpu.VMEM((frames * mem + 2, 2, tile, inner), jnp.bfloat16),
            pltpu.VMEM((2, (half + 2) * tile, inner), jnp.bfloat16),
            pltpu.VMEM((half + 2, tile, width), jnp.bfloat16),
            pltpu.VMEM((pieces, half, tile, wide), jnp.bfloat16),
            pltpu.VMEM((pieces, own, wide), jnp.bfloat16),
            pltpu.VMEM((pieces, own, wide), jnp.bfloat16),
            pltpu.VMEM((own, width), jnp.float32),
            pltpu.SMEM((frames * mem,), jnp.int32),
            pltpu.SMEM((count,), jnp.int32),
            pltpu.SemaphoreType.DMA((4,)),
            pltpu.SemaphoreType.DMA,
            pltpu.SemaphoreType.DMA,
            pltpu.SemaphoreType.DMA,
            pltpu.SemaphoreType.DMA,
            pltpu.SemaphoreType.DMA,
            pltpu.SemaphoreType.DMA((pieces,)),
            pltpu.SemaphoreType.DMA((pieces,)),
            pltpu.SemaphoreType.DMA((2,)),
            pltpu.SemaphoreType.DMA((2,)),
            pltpu.SemaphoreType.DMA,
            pltpu.SemaphoreType.DMA,
            pltpu.SemaphoreType.DMA((pieces,)),
            pltpu.SemaphoreType.DMA((pieces,)),
            pltpu.SemaphoreType.DMA((2,)),
            pltpu.SemaphoreType.DMA((2,)),
            pltpu.SemaphoreType.DMA((pieces,)),
            pltpu.SemaphoreType.DMA((pieces,)),
            pltpu.SemaphoreType.DMA((pieces,)),
            pltpu.SemaphoreType.DMA((pieces,)),
        ],
        compiler_params=pltpu.CompilerParams(
            collective_id=0, has_side_effects=True, vmem_limit_bytes=58 * 2**20
        ),
    )(
        memory_ids, memory_count, tile_mask.T, rows, cotangent.reshape(-1, width),
        w_query, w_out, w_key, w_value,
    )
    layer_out, latent_grad = pl.pallas_call(
        hand_over,
        in_specs=[vmem, vmem],
        out_specs=[vmem, vmem],
        out_shape=[jax.ShapeDtypeStruct((own, width), jnp.bfloat16)] * 2,
    )(layer_out, latent_grad)
    return (
        layer_out.reshape(frames, tile, width),
        latent_grad.reshape(frames, tile, width),
    )


def solution(mesh):
    placed = (
        P(("shard", "tm"), None, None),
        P(),
        P(),
        P(),
        P(),
        P(("shard", "tm"), None, None),
        P(("shard", "tm"), None),
        P(("shard", "tm")),
        P(("shard", "tm"), None),
    )
    return jax.shard_map(
        on_device,
        mesh=mesh,
        in_specs=placed,
        out_specs=(P(("shard", "tm"), None, None), P(("shard", "tm"), None, None)),
        check_vma=False,
    )
```

time: 87.5 us -> 81.5 us (0.931)
  local copies, waits for them, and re-layouts: 3.53 us -> 0 us
  Pallas kernels: 81.7 us -> 80.1 us
    pallas_call x1, Pallas kernels: 81.7 us -> 78.1 us  [on_device(): pl.pallas_call(functools.partial(layer_kernel, count, frames, mem, tile,...]
    unnamed x2 -> x0, local copies, waits for them, and re-layouts: 3.53 us -> none
    pallas_call x0 -> x1, Pallas kernels: none -> 2.02 us  [on_device(): pl.pallas_call(hand_over, in_specs=[vmem, vmem], out_specs=[vmem, vmem],...]
where the time goes in v3:
time: 81.5 us; the launch traced here: 80.8 us
  Pallas kernels  80.1 us (98%)
    pallas_call x1, Pallas kernels, on_device(): pl.pallas_call(functools.partial(layer_kernel, count, frames, mem, tile,...  78.1 us
    pallas_call x1, Pallas kernels, on_device(): pl.pallas_call(hand_over, in_specs=[vmem, vmem], out_specs=[vmem, vmem],...  2.02 us

profile of v3, /device:TPU:16, one launch (start us, length us, event | category | flops | bytes accessed | tf_op | source)
XLA Modules:
  0.0 80.8 jit_solution(2490305560686692831)
XLA Ops:
  0.6 78.1 %shard_map.104 = (bf16[128,1536]{1,0:T(8,128)(2,1)}, bf16[128,1536]{1,0:T(8,128)(2,1)}) custom-call(s32[4,4]{1,0:T(4,128)} %ids.1, s32[4]{0:T(128)} %recalled.1, s32[2,4]{1,0:T(2,128)} %bitcast.7, bf16[128,1536]{1,0:T(8,128)(2,1)} %bitcast.5, bf16[128,1536]{1,0:T(8,128)(2,1)} %bitcast.6, bf16[1536,1536]{1,0:T(8,128)(2,1)} %wq_hbm.1, ...), custom_call_target="tpu_custom_call" | custom-call | tf_op jit(solution)/shard_map/pallas_call | solution.py:493
  78.8 2.0 %shard_map.105 = (bf16[128,1536]{1,0:T(8,128)(2,1)}, bf16[128,1536]{1,0:T(8,128)(2,1)}) custom-call(bf16[128,1536]{1,0:T(8,128)(2,1)} %get-tuple-element.6.layer_in, bf16[128,1536]{1,0:T(8,128)(2,1)} %get-tuple-element.7.grad_in), custom_call_target="tpu_custom_call" | custom-call | tf_op jit(solution)/shard_map/pallas_call | solution.py:560

commit v4 on v3

--- a/solution.py
+++ b/solution.py
@@ -65,6 +65,8 @@
     def beside(side):
         return {"tm": lax.rem(me + (1 if side == 0 else count - 1), count)}
 
+    has_next = me < count - 1
+    has_last = me > 0
     barrier = pltpu.get_barrier_semaphore()
 
     @pl.loop(1, count)
@@ -129,8 +131,14 @@
 
     for p in range(pieces):
         swap(p).start()
-    push_halo(0).start()
-    push_halo(1).start()
+    @pl.when(has_next)
+    def _():
+        push_halo(0).start()
+
+    @pl.when(has_last)
+    def _():
+        push_halo(1).start()
+
     want_in[0] = want_out[0]
     mates = pl.ds(1, half - 1)
     pltpu.make_async_copy(want_in.at[mates], want_in.at[mates], want_recv).wait()
@@ -199,21 +207,11 @@
         lanes = pl.ds(pl.multiple_of(p * wide, wide), wide)
         g_ref[:, lanes] = dot(cot_ref[...], weights[1, lanes, :], NT).astype(jnp.bfloat16)
 
-    push_halo(0).wait_recv()
-    push_halo(1).wait_recv()
+    for p in range(1, pieces):
+        pick_far(p)
+
     loads[2].wait()
     loads[3].wait()
-
-    @pl.loop(0, pieces)
-    def _(p):
-        lanes = pl.ds(pl.multiple_of(p * wide, wide), wide)
-        ext = jnp.concatenate([rows_in[half], x_ref[...], rows_in[half + 1]], axis=0)
-        k_ext[:, lanes] = dot(ext, weights[2, :, lanes], NN).astype(jnp.bfloat16)
-        v_ext[:, lanes] = dot(ext, weights[3, :, lanes], NN).astype(jnp.bfloat16)
-
-    for p in range(1, pieces):
-        pick_far(p)
-
     mates_rows = rows_in.at[mates]
     pltpu.make_async_copy(mates_rows, mates_rows, row_recv).wait()
 
@@ -227,6 +225,30 @@
                 .astype(jnp.bfloat16)
                 .reshape(half, tile, wide)
             )
+
+    @pl.when(has_last)
+    def _():
+        push_halo(0).wait_recv()
+
+    @pl.when(has_next)
+    def _():
+        push_halo(1).wait_recv()
+
+    @pl.when(jnp.logical_not(has_last))
+    def _():
+        rows_in[half] = jnp.zeros((tile, width), rows_in.dtype)
+
+    @pl.when(jnp.logical_not(has_next))
+    def _():
+        rows_in[half + 1] = jnp.zeros((tile, width), rows_in.dtype)
+
+
+    @pl.loop(0, pieces)
+    def _(p):
+        lanes = pl.ds(pl.multiple_of(p * wide, wide), wide)
+        ext = jnp.concatenate([rows_in[half], x_ref[...], rows_in[half + 1]], axis=0)
+        k_ext[:, lanes] = dot(ext, weights[2, :, lanes], NN).astype(jnp.bfloat16)
+        v_ext[:, lanes] = dot(ext, weights[3, :, lanes], NN).astype(jnp.bfloat16)
 
     for piece in range(pieces):
         came = far_in.at[piece, mates]
@@ -283,31 +305,41 @@
         kept_at = pl.ds(pl.multiple_of(g * rows, rows), rows)
         held = [None, None]
         late = [None, None]
-        for f in range(frames):
-            here = slice(f * tile, (f + 1) * tile)
-            keys = gather(f, lanes, k_ext, k_mem)
-            values = gather(f, lanes, v_ext, v_mem)
-            queries = spread(q_ref[here, lanes] * scale)
-            grads = spread(g_ref[here, lanes])
-            scores = dot(keys, queries, NT)
+        keys = [gather(f, lanes, k_ext, k_mem) for f in range(frames)]
+        values = [gather(f, lanes, v_ext, v_mem) for f in range(frames)]
+        heres = [slice(f * tile, (f + 1) * tile) for f in range(frames)]
+        queries = [spread(q_ref[here, lanes] * scale) for here in heres]
+        grads = [spread(g_ref[here, lanes]) for here in heres]
+        raw = {}
+        prob_grads = {}
+        lows = {}
+        score_grads = {}
+
+        def multiply(f):
+            raw[f] = dot(keys[f], queries[f], NT)
+            prob_grads[f] = dot(values[f], grads[f], NT)
+
+        def soften(f):
             scores = jnp.concatenate(
                 [
                     part if bias is None else part + bias
-                    for bias, part in zip(hide(f), jnp.split(scores, 3 + mem, axis=0))
+                    for bias, part in zip(hide(f), jnp.split(raw[f], 3 + mem, axis=0))
                 ],
                 axis=0,
             )
             expo = jnp.exp(scores - jnp.max(scores, axis=0, keepdims=True))
             prob = expo * (1.0 / jnp.sum(expo, axis=0, keepdims=True))
-            low = prob.astype(jnp.bfloat16)
-            prob_grad = dot(values, grads, NT)
-            delta = jnp.sum(prob * prob_grad, axis=0, keepdims=True)
-            score_grad = (prob * (prob_grad - delta)).astype(jnp.bfloat16)
-            kept[0, f, :, kept_at] = low
-            kept[1, f, :, kept_at] = score_grad
+            lows[f] = prob.astype(jnp.bfloat16)
+            delta = jnp.sum(prob * prob_grads[f], axis=0, keepdims=True)
+            score_grads[f] = (prob * (prob_grads[f] - delta)).astype(jnp.bfloat16)
+            kept[0, f, :, kept_at] = lows[f]
+            kept[1, f, :, kept_at] = score_grads[f]
+
+        def spill(f):
+            here = heres[f]
             parts = (
-                dot(score_grad, queries, NN).astype(jnp.bfloat16),
-                dot(low, grads, NN).astype(jnp.bfloat16),
+                dot(score_grads[f], queries[f], NN).astype(jnp.bfloat16),
+                dot(lows[f], grads[f], NN).astype(jnp.bfloat16),
             )
             for kv, part in enumerate(parts):
                 before = part[0:tile]
@@ -329,6 +361,15 @@
                 for j in range(mem):
                     blocks[f * mem + j, kv, :, lanes] = part[(3 + j) * tile : (4 + j) * tile]
 
+        multiply(0)
+        for f in range(frames):
+            if f + 1 < frames:
+                multiply(f + 1)
+            soften(f)
+            if f > 0:
+                spill(f - 1)
+        spill(frames - 1)
+
     @pl.loop(0, steps)
     def _(g):
         attend(g)
@@ -415,8 +456,15 @@
             def _(i):
                 push_near(i).start()
 
-            push_edge(0).start()
-            push_edge(1).start()
+
+            @pl.when(has_next)
+            def _():
+                push_edge(0).start()
+
+            @pl.when(has_last)
+            def _():
+                push_edge(1).start()
+
             near_in[0] = rows_out[0]
 
     @pl.loop(0, steps)
@@ -434,8 +482,23 @@
 
     came = near_in.at[mates]
     pltpu.make_async_copy(came, came, near_recv).wait()
-    push_edge(0).wait_recv()
-    push_edge(1).wait_recv()
+
+    @pl.when(has_last)
+    def _():
+        push_edge(0).wait_recv()
+
+    @pl.when(has_next)
+    def _():
+        push_edge(1).wait_recv()
+
+    @pl.when(jnp.logical_not(has_last))
+    def _():
+        near_in[half] = jnp.zeros((tile, width), near_in.dtype)
+
+    @pl.when(jnp.logical_not(has_next))
+    def _():
+        near_in[half + 1] = jnp.zeros((tile, width), near_in.dtype)
+
     for p in range(pieces):
         lanes = cuts[p]
         total[:, lanes] += dot(
@@ -460,10 +523,16 @@
         pltpu.make_async_copy(gone, gone, back_send.at[p]).wait()
         swap(p).wait_send()
         relay(p).wait_send()
-    push_halo(0).wait_send()
-    push_halo(1).wait_send()
-    push_edge(0).wait_send()
-    push_edge(1).wait_send()
+
+    @pl.when(has_next)
+    def _():
+        push_halo(0).wait_send()
+        push_edge(0).wait_send()
+
+    @pl.when(has_last)
+    def _():
+        push_halo(1).wait_send()
+        push_edge(1).wait_send()
 
 
 def hand_over(layer_in, grad_in, layer_ref, grad_ref):

time: 81.5 us -> 75.6 us (0.928)
  Pallas kernels: 80.1 us -> 74.2 us
    pallas_call x1, Pallas kernels: 78.1 us -> 72.2 us  [on_device(): pl.pallas_call(functools.partial(layer_kernel, count, frames, mem, tile,...]
where the time goes in v4:
time: 75.6 us; the launch traced here: 74.8 us
  Pallas kernels  74.2 us (98%)
    pallas_call x1, Pallas kernels, on_device(): pl.pallas_call(functools.partial(layer_kernel, count, frames, mem, tile,...  72.2 us
    pallas_call x1, Pallas kernels, on_device(): pl.pallas_call(hand_over, in_specs=[vmem, vmem], out_specs=[vmem, vmem],...  2.02 us

profile of v4, /device:TPU:16, one launch (start us, length us, event | category | flops | bytes accessed | tf_op | source)
XLA Modules:
  0.0 74.8 jit_solution(3753300380683462791)
XLA Ops:
  0.6 72.2 %shard_map.104 = (bf16[128,1536]{1,0:T(8,128)(2,1)}, bf16[128,1536]{1,0:T(8,128)(2,1)}) custom-call(s32[4,4]{1,0:T(4,128)} %ids.1, s32[4]{0:T(128)} %recalled.1, s32[2,4]{1,0:T(2,128)} %bitcast.7, bf16[128,1536]{1,0:T(8,128)(2,1)} %bitcast.5, bf16[128,1536]{1,0:T(8,128)(2,1)} %bitcast.6, bf16[1536,1536]{1,0:T(8,128)(2,1)} %wq_hbm.1, ...), custom_call_target="tpu_custom_call" | custom-call | tf_op jit(solution)/shard_map/pallas_call | solution.py:562
  72.8 2.0 %shard_map.105 = (bf16[128,1536]{1,0:T(8,128)(2,1)}, bf16[128,1536]{1,0:T(8,128)(2,1)}) custom-call(bf16[128,1536]{1,0:T(8,128)(2,1)} %get-tuple-element.6.layer_in, bf16[128,1536]{1,0:T(8,128)(2,1)} %get-tuple-element.7.grad_in), custom_call_target="tpu_custom_call" | custom-call | tf_op jit(solution)/shard_map/pallas_call | solution.py:629

commit v5 on v4

--- a/solution.py
+++ b/solution.py
@@ -563,10 +563,7 @@
         functools.partial(layer_kernel, count, frames, mem, tile, head_dim, steps),
         in_specs=[smem] * 3 + [vmem] + [hbm] * 5,
         out_specs=[vmem, vmem],
-        out_shape=[
-            jax.ShapeDtypeStruct((own, width), jnp.bfloat16),
-            jax.ShapeDtypeStruct((own, width), jnp.bfloat16),
-        ],
+        out_shape=[pltpu.VMEM((own, width), jnp.bfloat16)] * 2,
         scratch_shapes=[
             pltpu.VMEM((4, width, inner), jnp.bfloat16),
             pltpu.VMEM((own, width), jnp.bfloat16),
@@ -631,7 +628,10 @@
         in_specs=[vmem, vmem],
         out_specs=[vmem, vmem],
         out_shape=[jax.ShapeDtypeStruct((own, width), jnp.bfloat16)] * 2,
-    )(layer_out, latent_grad)
+    )(
+        pltpu.with_memory_space_constraint(layer_out, pltpu.VMEM),
+        pltpu.with_memory_space_constraint(latent_grad, pltpu.VMEM),
+    )
     return (
         layer_out.reshape(frames, tile, width),
         latent_grad.reshape(frames, tile, width),

time: 75.6 us -> 73.6 us (0.974)
  Pallas kernels: 74.2 us -> 72.2 us
    pallas_call x1, Pallas kernels: 2.02 us -> 0.93 us  [on_device(): pl.pallas_call(hand_over, in_specs=[vmem, vmem], out_specs=[vmem, vmem],...]
    pallas_call x1, Pallas kernels: 72.2 us -> 71.3 us  [on_device(): pl.pallas_call(functools.partial(layer_kernel, count, frames, mem, tile,...]
where the time goes in v5:
time: 73.6 us; the launch traced here: 72.9 us
  Pallas kernels  72.2 us (98%)
    pallas_call x1, Pallas kernels, on_device(): pl.pallas_call(functools.partial(layer_kernel, count, frames, mem, tile,...  71.3 us

profile of v5, /device:TPU:16, one launch (start us, length us, event | category | flops | bytes accessed | tf_op | source)
XLA Modules:
  0.0 72.9 jit_solution(4560474721789050262)
XLA Ops:
  0.6 71.3 %shard_map.104 = (bf16[128,1536]{1,0:T(8,128)(2,1)S(1)}, bf16[128,1536]{1,0:T(8,128)(2,1)S(1)}) custom-call(s32[4,4]{1,0:T(4,128)} %ids.1, s32[4]{0:T(128)} %recalled.1, s32[2,4]{1,0:T(2,128)} %bitcast.7, bf16[128,1536]{1,0:T(8,128)(2,1)} %bitcast.5, bf16[128,1536]{1,0:T(8,128)(2,1)} %bitcast.6, bf16[1536,1536]{1,0:T(8,128)(2,1)} %wq_hbm.1, ...), custom_call_target="tpu_custom_call" | custom-call | tf_op jit(solution)/shard_map/pallas_call | solution.py:562
  71.9 0.9 %shard_map.105 = (bf16[128,1536]{1,0:T(8,128)(2,1)}, bf16[128,1536]{1,0:T(8,128)(2,1)}) custom-call(bf16[128,1536]{1,0:T(8,128)(2,1)S(1)} %get-tuple-element.6.layer_in, bf16[128,1536]{1,0:T(8,128)(2,1)S(1)} %get-tuple-element.7.grad_in), custom_call_target="tpu_custom_call" | custom-call | tf_op jit(solution)/shard_map/pallas_call | solution.py:626

commit v6 on v5

--- a/solution.py
+++ b/solution.py
@@ -22,13 +22,13 @@
 
 def layer_kernel(
     count, frames, mem, tile, head_dim, steps,
-    ids, recalled, tiles, x_ref, cot_hbm, wq_hbm, wo_hbm, wk_hbm, wv_hbm,
+    ids, recalled, tiles, x_hbm, cot_hbm, wq_hbm, wo_hbm, wk_hbm, wv_hbm,
     layer_ref, grad_ref,
-    weights, cot_ref, q_ref, g_ref, k_ext, v_ext, k_mem, v_mem, want_out, want_in, choose,
+    weights, x_ref, cot_ref, q_ref, g_ref, k_ext, v_ext, k_mem, v_mem, want_out, want_in, choose,
     rows_out, rows_in, far_out, far_in, x_far, far_sum, kept, mixed, query_grad, sums, blocks,
     gathered, near_in, back_in, relay_out, relay_in, total,
     spots, place,
-    weight_sem, cot_sem, want_send, want_recv, row_send, row_recv, far_send, far_recv,
+    weight_sem, x_sem, cot_sem, want_send, want_recv, row_send, row_recv, far_send, far_recv,
     halo_send, halo_recv, near_send, near_recv, back_send, back_recv, edge_send, edge_recv,
     swap_send, swap_recv, relay_send, relay_recv,
 ):
@@ -48,32 +48,35 @@
         pltpu.make_async_copy(source, weights.at[i], weight_sem.at[i])
         for i, source in enumerate((wq_hbm, wo_hbm, wk_hbm, wv_hbm))
     ]
+    load_x = pltpu.make_async_copy(x_hbm, x_ref, x_sem)
     load_cot = pltpu.make_async_copy(cot_hbm, cot_ref, cot_sem)
+    load_x.start()
+
+    def mate(i):
+        return {"tm": base + lax.rem(place_in + i, half)}
+
+    def asker(i):
+        return {"tm": base + lax.rem(place_in + half - i, half)}
+
+    partner = {"tm": lax.rem(me + half, count)}
+
+    def beside(side):
+        return {"tm": lax.rem(me + (1 if side == 0 else count - 1), count)}
+
+    has_next = me < count - 1
+    has_last = me > 0
+    barrier = pltpu.get_barrier_semaphore()
+
+    @pl.loop(1, count)
+    def _(i):
+        pl.semaphore_signal(
+            barrier, inc=1, device_id={"tm": lax.rem(me + i, count)}, device_id_type=MESH
+        )
+
     loads[0].start()
     load_cot.start()
     for load in loads[1:]:
         load.start()
-
-    def mate(i):
-        return {"tm": base + lax.rem(place_in + i, half)}
-
-    def asker(i):
-        return {"tm": base + lax.rem(place_in + half - i, half)}
-
-    partner = {"tm": lax.rem(me + half, count)}
-
-    def beside(side):
-        return {"tm": lax.rem(me + (1 if side == 0 else count - 1), count)}
-
-    has_next = me < count - 1
-    has_last = me > 0
-    barrier = pltpu.get_barrier_semaphore()
-
-    @pl.loop(1, count)
-    def _(i):
-        pl.semaphore_signal(
-            barrier, inc=1, device_id={"tm": lax.rem(me + i, count)}, device_id_type=MESH
-        )
 
     slots = []
     slot_at = lax.broadcasted_iota(jnp.int32, want_out.shape, 0)
@@ -90,6 +93,7 @@
         asked = jnp.where(slot_at == slot, lax.rem(frame, frames), asked)
     want_out[...] = asked
 
+    load_x.wait()
     pl.semaphore_wait(barrier, count - 1)
 
     def ask(i):
@@ -561,11 +565,12 @@
     hbm = pl.BlockSpec(memory_space=pl.ANY)
     layer_out, latent_grad = pl.pallas_call(
         functools.partial(layer_kernel, count, frames, mem, tile, head_dim, steps),
-        in_specs=[smem] * 3 + [vmem] + [hbm] * 5,
+        in_specs=[smem] * 3 + [hbm] * 6,
         out_specs=[vmem, vmem],
         out_shape=[pltpu.VMEM((own, width), jnp.bfloat16)] * 2,
         scratch_shapes=[
             pltpu.VMEM((4, width, inner), jnp.bfloat16),
+            pltpu.VMEM((own, width), jnp.bfloat16),
             pltpu.VMEM((own, width), jnp.bfloat16),
             pltpu.VMEM((own, inner), jnp.bfloat16),
             pltpu.VMEM((own, inner), jnp.bfloat16),
@@ -601,6 +606,7 @@
             pltpu.SemaphoreType.DMA,
             pltpu.SemaphoreType.DMA,
             pltpu.SemaphoreType.DMA,
+            pltpu.SemaphoreType.DMA,
             pltpu.SemaphoreType.DMA((pieces,)),
             pltpu.SemaphoreType.DMA((pieces,)),
             pltpu.SemaphoreType.DMA((2,)),

time: 73.6 us -> 73.2 us (level)
  no operation moved by 1% of the time
where the time goes in v6:
time: 73.2 us; the launch traced here: 72.5 us
  Pallas kernels  71.8 us (98%)
    pallas_call x1, Pallas kernels, on_device(): pl.pallas_call(functools.partial(layer_kernel, count, frames, mem, tile,...  70.9 us

profile of v6, /device:TPU:16, one launch (start us, length us, event | category | flops | bytes accessed | tf_op | source)
XLA Modules:
  0.0 72.5 jit_solution(1703802541503454233)
XLA Ops:
  0.6 70.9 %shard_map.104 = (bf16[128,1536]{1,0:T(8,128)(2,1)S(1)}, bf16[128,1536]{1,0:T(8,128)(2,1)S(1)}) custom-call(s32[4,4]{1,0:T(4,128)} %ids.1, s32[4]{0:T(128)} %recalled.1, s32[2,4]{1,0:T(2,128)} %bitcast.7, bf16[128,1536]{1,0:T(8,128)(2,1)} %bitcast.5, bf16[128,1536]{1,0:T(8,128)(2,1)} %bitcast.6, bf16[1536,1536]{1,0:T(8,128)(2,1)} %wq_hbm.1, ...), custom_call_target="tpu_custom_call" | custom-call | tf_op jit(solution)/shard_map/pallas_call | solution.py:566
  71.5 0.9 %shard_map.105 = (bf16[128,1536]{1,0:T(8,128)(2,1)}, bf16[128,1536]{1,0:T(8,128)(2,1)}) custom-call(bf16[128,1536]{1,0:T(8,128)(2,1)S(1)} %get-tuple-element.6.layer_in, bf16[128,1536]{1,0:T(8,128)(2,1)S(1)} %get-tuple-element.7.grad_in), custom_call_target="tpu_custom_call" | custom-call | tf_op jit(solution)/shard_map/pallas_call | solution.py:632

commit v7 on v5

--- a/solution.py
+++ b/solution.py
@@ -362,10 +362,11 @@
                     blocks[f * mem + j, kv, :, lanes] = part[(3 + j) * tile : (4 + j) * tile]
 
         multiply(0)
+        multiply(1)
         for f in range(frames):
-            if f + 1 < frames:
-                multiply(f + 1)
             soften(f)
+            if f + 2 < frames:
+                multiply(f + 2)
             if f > 0:
                 spill(f - 1)
         spill(frames - 1)

time: 73.6 us -> 72.6 us (0.986)
  Pallas kernels: 72.2 us -> 71.2 us
    pallas_call x1, Pallas kernels: 71.3 us -> 70.3 us  [on_device(): pl.pallas_call(functools.partial(layer_kernel, count, frames, mem, tile,...]
where the time goes in v7:
time: 72.6 us; the launch traced here: 71.9 us
  Pallas kernels  71.2 us (98%)
    pallas_call x1, Pallas kernels, on_device(): pl.pallas_call(functools.partial(layer_kernel, count, frames, mem, tile,...  70.3 us

profile of v7, /device:TPU:16, one launch (start us, length us, event | category | flops | bytes accessed | tf_op | source)
XLA Modules:
  0.0 71.9 jit_solution(1769137404103594727)
XLA Ops:
  0.6 70.3 %shard_map.104 = (bf16[128,1536]{1,0:T(8,128)(2,1)S(1)}, bf16[128,1536]{1,0:T(8,128)(2,1)S(1)}) custom-call(s32[4,4]{1,0:T(4,128)} %ids.1, s32[4]{0:T(128)} %recalled.1, s32[2,4]{1,0:T(2,128)} %bitcast.7, bf16[128,1536]{1,0:T(8,128)(2,1)} %bitcast.5, bf16[128,1536]{1,0:T(8,128)(2,1)} %bitcast.6, bf16[1536,1536]{1,0:T(8,128)(2,1)} %wq_hbm.1, ...), custom_call_target="tpu_custom_call" | custom-call | tf_op jit(solution)/shard_map/pallas_call | solution.py:563
  71.0 0.9 %shard_map.105 = (bf16[128,1536]{1,0:T(8,128)(2,1)}, bf16[128,1536]{1,0:T(8,128)(2,1)}) custom-call(bf16[128,1536]{1,0:T(8,128)(2,1)S(1)} %get-tuple-element.6.layer_in, bf16[128,1536]{1,0:T(8,128)(2,1)S(1)} %get-tuple-element.7.grad_in), custom_call_target="tpu_custom_call" | custom-call | tf_op jit(solution)/shard_map/pallas_call | solution.py:627
